TPU v7x, 256 devices: a whole 4x4x8 slice. The times are simulated.
256 devices in a mesh: dp: 32 (over z, x_hi, core), tensor: 8 (over x_lo, y).
Axes of the slice: x: 4 (x_hi: 2, x_lo: 2; x = x_hi * 2 + x_lo), y: 4, z: 8, core: 2. Of those that a mesh axis runs over, the one named last changes fastest.
Arguments:
- tokens: bfloat16 [8192, 8192], P('dp', 'tensor'), may hold values from -6 to 6
- out_grad: bfloat16 [8192, 8, 256], P('dp', 'tensor'), may hold values from -2 to 2
- active: int32 [32, 8, 2], P('dp', 'tensor'), may hold values from 0 to 28, as said below
- w_gate: bfloat16 [8192, 28672], P('dp', 'tensor'), may hold values from -0.0625 to 0.0625
- w_up: bfloat16 [8192, 28672], P('dp', 'tensor'), may hold values from -0.0625 to 0.0625
Outputs:
- input_grad: bfloat16 [8192, 8192], P('dp', 'tensor')
- gate_weight_grad: bfloat16 [8192, 28672], P('dp', 'tensor')
- up_weight_grad: bfloat16 [8192, 28672], P('dp', 'tensor')
Inputs may be any that keep to these rules, and one draw needn't show every extreme that they name: `active`: each entry is a block number of the shard or 28 for an empty slot. In every tile and shard the live entries come first, are distinct and number at least one; in every tile some shard has all 2 slots live.
All inputs are finite; a program needn't handle non-finite values.
Results may differ from a plain program's by a relative error of at most 0.014.
Values may be sent and summed in bfloat16 or wider, within the bound.
A program may use at most 128 MiB of HBM per device.

v0:
```python
import jax
import jax.numpy as jnp
from jax import lax
from jax.sharding import PartitionSpec as P

BLOCK = 128
TILE = 256
CAP = 2


def copy_for_each(array, axis):
    length = lax.axis_size(axis)
    return lax.all_to_all(
        jnp.broadcast_to(array[None], (length, *array.shape)), axis, 0, 0, tiled=True
    )


def in_order(parts, dim):
    parts = jnp.moveaxis(parts, 0, dim)
    lengths = parts.shape
    return parts.reshape(*lengths[:dim], lengths[dim] * lengths[dim + 1], *lengths[dim + 2 :])


def gather_directly(array, axis, dim):
    parts = copy_for_each(array, axis)
    return in_order(parts, dim)


def sent_together(arrays, axis, split_dim, concat_dim, along):
    widths = [a.shape[along] for a in arrays]
    both = jnp.concatenate(arrays, axis=along)
    result = lax.all_to_all(both, axis, split_axis=split_dim, concat_axis=concat_dim, tiled=True)
    return tuple(jnp.split(result, [sum(widths[:k]) for k in range(1, len(widths))], axis=along))


def in_one_piece(arrays, axis, dim, along):
    ends, at = ([], 0)
    for a in arrays[:-1]:
        at += a.shape[along]
        ends.append(at)
    both = jnp.concatenate(arrays, axis=along)
    return tuple(jnp.split(lax.all_gather(both, axis, axis=dim, tiled=True), ends, axis=along))


def per_device(tokens, out_grad, active, w_gate, w_up):
    row_count = tokens.shape[0]
    tiles_here = active.shape[0]
    blocks = w_gate.shape[1] // BLOCK
    rows_local = w_gate.shape[0]
    gathered = lax.all_gather(tokens, "tensor", axis=1, tiled=True)
    full_width = gathered.shape[1]
    listed = gather_directly(active, "dp", 0)
    peer_count = lax.axis_size("dp")
    slot_count = tiles_here * CAP
    wanted = jnp.minimum(listed.reshape(peer_count, slot_count), blocks - 1)
    gate_send = jnp.take(w_gate.reshape(rows_local, blocks, BLOCK), wanted, axis=1).reshape(
        rows_local, peer_count, slot_count * BLOCK
    )
    up_send = jnp.take(w_up.reshape(rows_local, blocks, BLOCK), wanted, axis=1).reshape(
        rows_local, peer_count, slot_count * BLOCK
    )
    gate_cols, up_cols = sent_together((gate_send, up_send), "dp", 1, 0, 2)
    tile_tokens = gathered.reshape(tiles_here, TILE, full_width)
    gate_value = jnp.einsum(
        "tnd,dtc->tnc", tile_tokens, gate_cols, preferred_element_type=jnp.float32
    )
    up_value = jnp.einsum("tnd,dtc->tnc", tile_tokens, up_cols, preferred_element_type=jnp.float32)
    alive = (active.reshape(tiles_here, 1, CAP, 1) < blocks).astype(jnp.float32)
    alive_mask = jnp.broadcast_to(alive, (tiles_here, 1, CAP, BLOCK)).reshape(
        tiles_here, 1, CAP * BLOCK
    )
    upstream = out_grad.reshape(tiles_here, TILE, CAP * BLOCK).astype(jnp.float32)
    positive = jnp.maximum(gate_value, 0.0)
    gate_grad = (upstream * up_value * 2.0 * positive * alive_mask).astype(jnp.bfloat16)
    up_grad = (upstream * positive * positive * alive_mask).astype(jnp.bfloat16)
    partial_value = jnp.einsum(
        "tnc,dtc->tnd", gate_grad, gate_cols, preferred_element_type=jnp.float32
    )
    partial_value = partial_value + jnp.einsum(
        "tnc,dtc->tnd", up_grad, up_cols, preferred_element_type=jnp.float32
    )
    summed = lax.psum_scatter(
        partial_value.reshape(row_count, full_width).astype(jnp.bfloat16),
        "tensor",
        scatter_dimension=1,
        tiled=True,
    )
    row_slices = lax.all_to_all(gathered, "dp", split_axis=1, concat_axis=0, tiled=True)
    slices_tiled = row_slices.reshape(peer_count * tiles_here, TILE, rows_local)
    gate_all, up_all = in_one_piece((gate_grad, up_grad), "dp", 0, 1)
    gate_terms = jnp.einsum(
        "tnr,tnc->rtc", slices_tiled, gate_all, preferred_element_type=jnp.float32
    ).astype(jnp.bfloat16)
    up_terms = jnp.einsum(
        "tnr,tnc->rtc", slices_tiled, up_all, preferred_element_type=jnp.float32
    ).astype(jnp.bfloat16)
    gate_terms = gate_terms.reshape(rows_local, peer_count * slot_count, BLOCK)
    up_terms = up_terms.reshape(rows_local, peer_count * slot_count, BLOCK)
    placing = (
        listed.reshape(peer_count * slot_count, 1) == jnp.arange(blocks, dtype=jnp.int32)[None, :]
    ).astype(jnp.bfloat16)
    gate_weight_grad = jnp.einsum(
        "rsk,sb->rbk", gate_terms, placing, preferred_element_type=jnp.float32
    )
    up_weight_grad = jnp.einsum(
        "rsk,sb->rbk", up_terms, placing, preferred_element_type=jnp.float32
    )
    gate_weight_grad = gate_weight_grad.reshape(rows_local, blocks * BLOCK).astype(jnp.bfloat16)
    up_weight_grad = up_weight_grad.reshape(rows_local, blocks * BLOCK).astype(jnp.bfloat16)
    return (summed, gate_weight_grad, up_weight_grad)


def solution(mesh):
    placed = (
        P("dp", "tensor"),
        P("dp", "tensor", None),
        P("dp", "tensor", None),
        P("dp", "tensor"),
        P("dp", "tensor"),
    )
    return jax.shard_map(
        per_device,
        mesh=mesh,
        in_specs=placed,
        out_specs=(P("dp", "tensor"), P("dp", "tensor"), P("dp", "tensor")),
        check_vma=False,
    )
```

profile of v0, /device:TPU:7, one launch (start us, length us, event | category | flops | bytes accessed | tf_op | source)
XLA Modules:
  0.0 466.9 jit_solution(7106860521796707381)
XLA Ops:
  7.2 1.3 broadcast_in_dim.26
  8.4 11.9 %all-to-all-start = ((s32[32,1,1,2]{3,2,1,0:T(1,128)}), s32[32,1,1,2]{3,2,1,0:T(1,128)S(1)}, u32[]{:S(2)}, u32[]{:S(2)}) async-start(s32[32,1,1,2]{3,2,1,0:T(1,128)} %broadcast_in_dim.26), calls=%async_computation | async-start | bytes 32768 | tf_op jit(solution)/shard_map/all_to_all | solution.py:13
  20.3 3.8 copy.61
  24.1 2.9 copy.63
  27.0 3.8 copy.66
  30.8 3.8 copy.68
  34.6 0.1 copy.59
  34.7 0.1 copy.62
  34.8 0.1 reshape.130
  34.9 0.1 copy.60
  35.1 3.1 gather_fusion
  38.1 4.6 gather_fusion.1
  42.7 3.9 select_bitcast_fusion.1
  46.6 5.0 %copy_bitcast_fusion = (bf16[256,32,256]{2,0,1:T(8,128)(2,1)}, bf16[256,32,256]{2,0,1:T(8,128)(2,1)}) fusion(bf16[32,2,32,8,128]{4,3,2,1,0:T(8,128)(2,1)S(1)} %get-tuple-element.14, bf16[32,2,32,8,128]{4,3,2,1,0:T(8,128)(2,1)S(1)} %get-tuple-element.13), kind=kLoop, calls=%fused_computation.5 | loop fusion | bytes 16777216 | tf_op jit(solution)/shard_map/reshape | solution.py:59
  51.6 7.5 %pad_maximum_fusion = bf16[256,32,512]{2,0,1:T(8,128)(2,1)} fusion(bf16[256,32,256]{2,0,1:T(8,128)(2,1)} %get-tuple-element.17, bf16[256,32,256]{2,0,1:T(8,128)(2,1)} %get-tuple-element.18), kind=kLoop, calls=%fused_computation.4 | loop fusion | flops 16777216 | bytes 16777216 | tf_op jit(solution)/shard_map/concatenate | solution.py:31
  59.1 10.0 %all-to-all-start.1 = ((bf16[256,32,512]{2,0,1:T(8,128)(2,1)}), bf16[256,32,512]{2,0,1:T(8,128)(2,1)}, u32[]{:S(2)}, u32[]{:S(2)}) async-start(bf16[256,32,512]{2,0,1:T(8,128)(2,1)} %pad_maximum_fusion), calls=%async_computation.1 | async-start | bytes 16777216 | tf_op jit(solution)/shard_map/all_to_all | solution.py:32
  69.1 0.0 all-gather.3.cloned.1.call-start
  69.1 1.0 copy.70
  70.1 0.0 all-gather.3.cloned.1.call-update
  70.2 0.0 all-gather.5.cloned.1.call-start
  70.2 0.1 broadcast_bitcast_fusion
  70.3 92.6 %all-gather.3.cloned.1.call-done = bf16[256,8192]{0,1:T(8,128)(2,1)} async-done(((bf16[256,1024]{0,1:T(8,128)(2,1)}), bf16[256,8192]{0,1:T(8,128)(2,1)}) %all-gather.3.cloned.1.call-update) | async-done | bytes 4194320 | tf_op jit(solution)/shard_map/all_gather | solution.py:50
  162.9 88.4 %all-to-all-done.1 = bf16[256,32,512]{2,0,1:T(8,128)(2,1)} async-done(((bf16[256,32,512]{2,0,1:T(8,128)(2,1)}), bf16[256,32,512]{2,0,1:T(8,128)(2,1)}, u32[]{:S(2)}, u32[]{:S(2)}) %all-to-all-start.1) | async-done | bytes 8388640 | tf_op jit(solution)/shard_map/all_to_all | solution.py:32
  251.3 5.3 %fusion.29 = (bf16[256,256]{1,0:T(8,128)(2,1)S(1)}, f32[256,256]{1,0:T(8,128)S(1)}) fusion(bf16[256,1,256]{2,0,1:T(8,128)(2,1)S(1)} %copy-done.3, f32[256]{0:T(256)S(1)} %broadcast_bitcast_fusion, bf16[256,8192]{0,1:T(8,128)(2,1)} %all-gather.3.cloned.1.call-done, bf16[8192,1,512]{2,0,1:T(8,128)(2,1)} %bitcast.11), kind=kOutput, calls=%fused_computation.34 | convolution fusion | flops 1074135040 | bytes 8913920 | tf_op jit(solution)/shard_map/tnd,dtc->tnc/dot_general | solution.py:64
  256.7 4.0 fusion.27
  260.7 0.7 pad_maximum_fusion.1
  261.4 0.0 all-gather.5.cloned.1.call-update
  261.4 6.5 %copy.72 = bf16[256,32,256]{2,0,1:T(8,128)(2,1)} copy(bf16[256,32,256]{0,2,1:T(8,128)(2,1)} %bitcast.113) | data formatting | bytes 8388608 | tf_op jit(solution)/shard_map/all_to_all | solution.py:88
  267.9 9.6 %all-to-all-start.2 = ((bf16[256,32,256]{2,0,1:T(8,128)(2,1)}), bf16[256,32,256]{2,0,1:T(8,128)(2,1)}, u32[]{:S(2)}, u32[]{:S(2)}) async-start(bf16[256,32,256]{2,0,1:T(8,128)(2,1)} %copy.72), calls=%async_computation.3 | async-start | bytes 8388608 | tf_op jit(solution)/shard_map/all_to_all | solution.py:88
  277.6 0.2 reduce-scatter.2.cloned.1.call-start
  277.8 3.5 fusion.8
  281.3 5.6 %fusion = bf16[256,8192]{1,0:T(8,128)(2,1)} fusion(f32[256,8192]{1,0:T(8,128)S(1)} %fusion.8, bf16[256,256]{1,0:T(8,128)(2,1)S(1)} %get-tuple-element.15, bf16[8192,1,512]{2,0,1:T(8,128)(2,1)} %bitcast.11), kind=kOutput, calls=%fused_computation.3 | convolution fusion | flops 1077936128 | bytes 16908288 | tf_op jit(solution)/shard_map/tnc,dtc->tnd/dot_general | solution.py:79
  286.9 0.5 broadcast.50
  287.4 0.7 reduce.3
  288.1 0.1 eq.15
  288.2 104.4 %all-to-all-done.2 = bf16[256,32,256]{2,0,1:T(8,128)(2,1)} async-done(((bf16[256,32,256]{2,0,1:T(8,128)(2,1)}), bf16[256,32,256]{2,0,1:T(8,128)(2,1)}, u32[]{:S(2)}, u32[]{:S(2)}) %all-to-all-start.2) | async-done | bytes 4194336 | tf_op jit(solution)/shard_map/all_to_all | solution.py:88
  392.6 12.1 %all-gather.5.cloned.1.call-done = bf16[32,512,256]{2,1,0:T(8,128)(2,1)} async-done(((bf16[1,512,256]{2,1,0:T(8,128)(2,1)}), bf16[32,512,256]{2,1,0:T(8,128)(2,1)}) %all-gather.5.cloned.1.call-update) | async-done | bytes 8388624 | tf_op jit(solution)/shard_map/all_gather | solution.py:42
  404.7 6.8 %fusion.10 = bf16[32,256,256]{2,1,0:T(8,128)(2,1)} fusion(bf16[256,32,256]{2,0,1:T(8,128)(2,1)} %all-to-all-done.2, bf16[32,512,256]{2,1,0:T(8,128)(2,1)} %all-gather.5.cloned.1.call-done), kind=kOutput, calls=%fused_computation.20 | convolution fusion | flops 1075838976 | bytes 12582912 | tf_op jit(solution)/shard_map/tnr,tnc->rtc/dot_general | solution.py:91
  411.5 6.5 %copy.73 = bf16[256,64,128]{2,1,0:T(8,128)(2,1)} copy(bf16[256,64,128]{0,2,1:T(8,128)(2,1)} %bitcast.108) | data formatting | bytes 8388608 | tf_op jit(solution)/shard_map/reshape | solution.py:97
  418.0 2.9 convert_bitcast_fusion.1
  420.9 2.6 copy.74
  423.6 3.8 copy.78
  427.4 6.8 %fusion.15 = bf16[32,256,256]{2,1,0:T(8,128)(2,1)} fusion(bf16[256,32,256]{2,0,1:T(8,128)(2,1)} %all-to-all-done.2, bf16[32,512,256]{2,1,0:T(8,128)(2,1)} %all-gather.5.cloned.1.call-done), kind=kOutput, calls=%fused_computation.21 | convolution fusion | flops 1075838976 | bytes 12582912 | tf_op jit(solution)/shard_map/tnr,tnc->rtc/dot_general | solution.py:94
  434.2 6.6 %copy.76 = bf16[256,64,128]{2,1,0:T(8,128)(2,1)} copy(bf16[256,64,128]{0,2,1:T(8,128)(2,1)} %bitcast.107) | data formatting | bytes 8388608 | tf_op jit(solution)/shard_map/reshape | solution.py:98
  440.8 2.9 convert_bitcast_fusion
  443.7 2.7 copy.77
  446.4 3.8 copy.79
  450.2 10.1 %reduce-scatter.2.cloned.1.call-done = bf16[256,1024]{1,0:T(8,128)(2,1)} async-done(((bf16[256,8192]{1,0:T(8,128)(2,1)}), bf16[256,1024]{1,0:T(8,128)(2,1)}) %reduce-scatter.2.cloned.1.call-update) | async-done | bytes 524304 | tf_op jit(solution)/shard_map/reduce_scatter | solution.py:82
  (14 shorter events, 0.1 us)
Async XLA Ops:
  8.4 26.2 %all-to-all-start = ((s32[32,1,1,2]{3,2,1,0:T(1,128)}), s32[32,1,1,2]{3,2,1,0:T(1,128)S(1)}, u32[]{:S(2)}, u32[]{:S(2)}) async-start(s32[32,1,1,2]{3,2,1,0:T(1,128)} %broadcast_in_dim.26), calls=%async_computation | async-start | bytes 32768 | tf_op jit(solution)/shard_map/all_to_all | solution.py:13
  59.1 10.0 %copy-start.1 = (bf16[256,1024]{1,0:T(8,128)(2,1)S(1)}, bf16[256,1024]{1,0:T(8,128)(2,1)}, u32[]{:S(2)}) copy-start(bf16[256,1024]{1,0:T(8,128)(2,1)} %param.7) | copy-start | bytes 1572868
  59.1 11.1 %copy-start.2 = (s32[1,1,2]{2,1,0:T(1,128)S(1)}, s32[1,1,2]{2,1,0:T(1,128)}, u32[]{:S(2)}) copy-start(s32[1,1,2]{2,1,0:T(1,128)} %param.9) | copy-start | bytes 28
  59.1 192.2 %copy-start.3 = (bf16[256,1,256]{2,0,1:T(8,128)(2,1)S(1)}, bf16[256,1,256]{2,0,1:T(8,128)(2,1)}, u32[]{:S(2)}) copy-start(bf16[256,1,256]{2,0,1:T(8,128)(2,1)} %param.8) | copy-start | bytes 393220
  59.1 192.2 %all-to-all-start.1 = ((bf16[256,32,512]{2,0,1:T(8,128)(2,1)}), bf16[256,32,512]{2,0,1:T(8,128)(2,1)}, u32[]{:S(2)}, u32[]{:S(2)}) async-start(bf16[256,32,512]{2,0,1:T(8,128)(2,1)} %pad_maximum_fusion), calls=%async_computation.1 | async-start | bytes 16777216 | tf_op jit(solution)/shard_map/all_to_all | solution.py:32
  69.1 93.9 %all-gather.3.cloned.1.call-start = ((), (), s32[]{:S(2)}) async-start(), calls=%async_computation.4 | async-start | bytes 4718592 | tf_op jit(solution)/shard_map/all_gather | solution.py:50
  70.2 334.6 %all-gather.5.cloned.1.call-start = ((), (), s32[]{:S(2)}) async-start(), calls=%async_computation.6 | async-start | bytes 8650752 | tf_op jit(solution)/shard_map/all_gather | solution.py:42
  251.3 5.4 %copy-start = (bf16[256,8192]{0,1:T(8,128)(2,1)S(1)}, bf16[256,8192]{0,1:T(8,128)(2,1)}, u32[]{:S(2)}) copy-start(bf16[256,8192]{0,1:T(8,128)(2,1)} %all-gather.3.cloned.1.call-done) | copy-start | bytes 12582916
  267.9 124.7 %all-to-all-start.2 = ((bf16[256,32,256]{2,0,1:T(8,128)(2,1)}), bf16[256,32,256]{2,0,1:T(8,128)(2,1)}, u32[]{:S(2)}, u32[]{:S(2)}) async-start(bf16[256,32,256]{2,0,1:T(8,128)(2,1)} %copy.72), calls=%async_computation.3 | async-start | bytes 8388608 | tf_op jit(solution)/shard_map/all_to_all | solution.py:88
  277.6 182.8 %reduce-scatter.2.cloned.1.call-start = ((), (), s32[]{:S(2)}) async-start(), calls=%async_computation.5 | async-start | bytes 4718592 | tf_op jit(solution)/shard_map/reduce_scatter | solution.py:82
Sparse Core Ops, SparseCore 0:
  72.3 90.6 all-gather.2
  261.5 143.1 all-gather.4
  407.9 52.4 reduce-scatter.1
where the time goes:
time: 470 us; the launch traced here: 467 us
  waiting for transfers between devices  308 us (66%)
  local copies, waits for them, and re-layouts  62.8 us (13%)
  matrix products  37.8 us (8%)
  starting transfers between devices  31.8 us (7%)
  between operations  13.9 us (3%)
  other arithmetic  12.9 us (3%)
    all_to_all x1, waiting for transfers between devices, per_device(): lax.all_to_all(gathered, 'dp', split_axis=1, concat_axis=0, tiled=True)  104 us
    all_gather x1, waiting for transfers between devices, per_device(): gathered = lax.all_gather(tokens, 'tensor', axis=1, tiled=True)  92.6 us
    all_to_all x1, waiting for transfers between devices, sent_together(): lax.all_to_all(both, axis, split_axis=split_dim, concat_axis=concat_dim,...  88.4 us
    unnamed x13, local copies, waits for them, and re-layouts  16.2 us
    all_gather x1, waiting for transfers between devices, in_one_piece(): lax.all_gather(both, axis, axis=dim, tiled=True)  12.1 us
    all_to_all x1, starting transfers between devices, copy_for_each(): lax.all_to_all(jnp.broadcast_to(array[None], (length, *array.shape)), axi...  11.9 us
    reduce_scatter x1, waiting for transfers between devices, per_device(): lax.psum_scatter(partial_value.reshape(row_count, full_width).astype(jnp....  10.1 us
    all_to_all x1, starting transfers between devices, sent_together(): lax.all_to_all(both, axis, split_axis=split_dim, concat_axis=concat_dim,...  9.96 us
  transfers between devices with their start and end apart: 6, of which 5 were waited for; matrix products, arithmetic and copies ran while one was open for 17% of the time, Pallas kernels for 0%

commit v1 on v0

v1 whole, which is shorter than its diff:
```python
import jax
import jax.numpy as jnp
from jax import lax
from jax.experimental import pallas as pl
from jax.experimental.pallas import tpu as pltpu
from jax.sharding import PartitionSpec as P

BLOCK = 128
TILE = 256
CAP = 2


def block_columns(w_ref, block):
    return w_ref[:, pl.ds(pl.multiple_of(block * BLOCK, BLOCK), BLOCK)]


def listed_weights(listed, tile, blocks, gate_ref, up_ref):
    picked = [jnp.minimum(listed[tile * CAP + c], blocks - 1) for c in range(CAP)]
    columns = [block_columns(ref, b) for ref in (gate_ref, up_ref) for b in picked]
    return picked, jnp.concatenate(columns, axis=1)


def forward_kernel(listed, tok_ref, gate_ref, up_ref, out_ref):
    blocks = gate_ref.shape[1] // BLOCK
    _, weights = listed_weights(listed, pl.program_id(0), blocks, gate_ref, up_ref)
    rows = gate_ref.shape[0]
    tok = tok_ref[...].reshape(TILE, rows)
    out_ref[0] = jnp.dot(tok, weights, preferred_element_type=jnp.float32).astype(out_ref.dtype)


def backward_kernel(listed, tok_ref, grad_ref, gate_ref, up_ref, part_ref, dgate_ref, dup_ref, gate_acc, up_acc):
    blocks = gate_ref.shape[1] // BLOCK
    tile = pl.program_id(0)
    rows = gate_ref.shape[0]

    @pl.when(tile == 0)
    def _():
        gate_acc[...] = jnp.zeros_like(gate_acc)
        up_acc[...] = jnp.zeros_like(up_acc)

    picked, weights = listed_weights(listed, tile, blocks, gate_ref, up_ref)
    tok = tok_ref[...].reshape(TILE, rows)
    grads = grad_ref[0]
    part = lax.dot_general(grads, weights, (((1,), (1,)), ((), ())), preferred_element_type=jnp.float32)
    part_ref[...] = part.astype(part_ref.dtype).reshape(part_ref.shape)
    pieces = lax.dot_general(tok, grads, (((0,), (0,)), ((), ())), preferred_element_type=jnp.float32)
    pieces = pieces.astype(jnp.bfloat16).astype(jnp.float32)
    for k, acc in enumerate((gate_acc, up_acc)):
        for c in range(CAP):
            at = pl.ds(pl.multiple_of(picked[c] * BLOCK, BLOCK), BLOCK)
            acc[:, at] += pieces[:, (k * CAP + c) * BLOCK : (k * CAP + c + 1) * BLOCK]

    @pl.when(tile == pl.num_programs(0) - 1)
    def _():
        dgate_ref[...] = gate_acc[...].astype(dgate_ref.dtype)
        dup_ref[...] = up_acc[...].astype(dup_ref.dtype)


def per_device(tokens, out_grad, active, w_gate, w_up):
    dp, tp = lax.axis_size("dp"), lax.axis_size("tensor")
    rows, width = w_gate.shape
    blocks = width // BLOCK
    share = TILE // tp
    quarter = tokens.shape[1] // rows
    units = 2 * CAP * BLOCK

    listed = lax.all_gather(active.reshape(CAP), "dp", axis=0, tiled=True)

    spread = lax.all_to_all(tokens.reshape(tp, share, -1), "tensor", 0, 0, tiled=True)
    spread = spread.reshape(tp, share, quarter, rows).swapaxes(1, 2).reshape(dp, share, rows)
    mine = lax.all_to_all(spread, "dp", 0, 0, tiled=True)
    toks = lax.all_gather(mine, "tensor", axis=0)

    whole = pl.BlockSpec((rows, width), lambda q, *_: (0, 0))
    tok_spec = pl.BlockSpec((tp, 1, share, rows), lambda q, *_: (0, q, 0, 0))
    tile_spec = pl.BlockSpec((1, TILE, units), lambda q, *_: (q, 0, 0))
    partial = pl.pallas_call(
        forward_kernel,
        grid_spec=pltpu.PrefetchScalarGridSpec(
            num_scalar_prefetch=1, grid=(dp,), in_specs=[tok_spec, whole, whole], out_specs=tile_spec
        ),
        out_shape=jax.ShapeDtypeStruct((dp, TILE, units), jnp.bfloat16),
        compiler_params=pltpu.CompilerParams(vmem_limit_bytes=40 * 2**20),
    )(listed, toks, w_gate, w_up)
    both = lax.psum_scatter(partial, "dp", scatter_dimension=0, tiled=True)[0].astype(jnp.float32)

    gate, up = both[:, : CAP * BLOCK], both[:, CAP * BLOCK :]
    live = (active.reshape(1, CAP, 1) < blocks).astype(jnp.float32)
    live = jnp.broadcast_to(live, (1, CAP, BLOCK)).reshape(1, CAP * BLOCK)
    g = out_grad.reshape(TILE, CAP * BLOCK).astype(jnp.float32)
    relu = jnp.maximum(gate, 0.0)
    gate_grad = (g * up * 2.0 * relu * live).astype(jnp.bfloat16)
    up_grad = (g * relu * relu * live).astype(jnp.bfloat16)
    grads = lax.all_gather(jnp.concatenate([gate_grad, up_grad], axis=1), "dp", axis=0)

    parts, dgate, dup = pl.pallas_call(
        backward_kernel,
        grid_spec=pltpu.PrefetchScalarGridSpec(
            num_scalar_prefetch=1,
            grid=(dp,),
            in_specs=[tok_spec, tile_spec, whole, whole],
            out_specs=[tok_spec, whole, whole],
            scratch_shapes=[pltpu.VMEM((rows, width), jnp.float32)] * 2,
        ),
        out_shape=[
            jax.ShapeDtypeStruct((tp, dp, share, rows), jnp.bfloat16),
            jax.ShapeDtypeStruct((rows, width), jnp.bfloat16),
            jax.ShapeDtypeStruct((rows, width), jnp.bfloat16),
        ],
        compiler_params=pltpu.CompilerParams(vmem_limit_bytes=50 * 2**20),
    )(listed, toks, grads, w_gate, w_up)
    summed = lax.psum_scatter(parts, "tensor", scatter_dimension=0, tiled=True)[0]
    back = lax.all_to_all(summed, "dp", 0, 0, tiled=True)
    back = back.reshape(tp, quarter, share, rows).swapaxes(1, 2).reshape(tp, share, quarter * rows)
    input_grad = lax.all_to_all(back, "tensor", 0, 0, tiled=True).reshape(TILE, quarter * rows)
    return input_grad, dgate, dup


def solution(mesh):
    placed = (
        P("dp", "tensor"),
        P("dp", "tensor", None),
        P("dp", "tensor", None),
        P("dp", "tensor"),
        P("dp", "tensor"),
    )
    return jax.shard_map(
        per_device,
        mesh=mesh,
        in_specs=placed,
        out_specs=(P("dp", "tensor"), P("dp", "tensor"), P("dp", "tensor")),
        check_vma=False,
    )
```

time: 470 us -> 507 us (1.079)
  blocking collectives: 0 us -> 91.3 us
  local copies, waits for them, and re-layouts: 62.8 us -> 7.59 us
  Pallas kernels: 0 us -> 43.1 us
  matrix products: 37.8 us -> 0 us
  waiting for transfers between devices: 308 us -> 345 us
  starting transfers between devices: 31.8 us -> 0.16 us
  other arithmetic: 12.9 us -> 1.85 us
    all_to_all x3 -> x0, waiting for transfers between devices: 193 us -> none  [the longest x1 104 us: per_device(): lax.all_to_all(gathered, 'dp', split_axis=1, concat_axis=0, tiled=True)]
    reduce_scatter x1 -> x2, waiting for transfers between devices: 10.1 us -> 201 us  [the longest x1 148 us: per_device(): lax.psum_scatter(partial, 'dp', scatter_dimension=0, tiled=True)[0]]
    all_to_all x0 -> x4, blocking collectives: none -> 80.7 us  [the longest x1 29.9 us: per_device(): mine = lax.all_to_all(spread, 'dp', 0, 0, tiled=True)]
    pallas_call x0 -> x2, Pallas kernels: none -> 43.1 us  [the longest x1 27 us: per_device(): pl.pallas_call(backward_kernel, grid_spec=pltpu.PrefetchScalarGridSpec(nu...]
    all_gather x2, waiting for transfers between devices: 105 us -> 144 us  [the longest x1 106 us: per_device(): lax.all_gather(jnp.concatenate([gate_grad, up_grad], axis=1), 'dp', axis=0)]
    dot_general x8 -> x0, matrix products: 37.8 us -> none  [the longest x1 6.84 us: per_device(): jnp.einsum('tnr,tnc->rtc', slices_tiled, up_all, preferred_element_type=j...]
    all_to_all x3 -> x0, starting transfers between devices: 31.5 us -> none  [the longest x1 11.9 us: copy_for_each(): lax.all_to_all(jnp.broadcast_to(array[None], (length, *array.shape)), axi...]
    reshape x5 -> x2, local copies, waits for them, and re-layouts: 24.8 us -> 0.78 us  [per_device(): back.reshape(tp, quarter, share, rows).swapaxes(1, 2)]
  transfers between devices with their start and end apart: 6 -> 4, of which waited for: 5 -> 4; matrix products, arithmetic and copies ran while one was open for 17% -> 0% of each run, Pallas kernels for 0% -> 0%
where the time goes in v1:
time: 507 us; the launch traced here: 503 us
  waiting for transfers between devices  345 us (68%)
  blocking collectives  91.3 us (18%)
  Pallas kernels  43.1 us (9%)
  between operations  14.5 us (3%)
  local copies, waits for them, and re-layouts  7.59 us (1%)
    reduce_scatter x1, waiting for transfers between devices, per_device(): lax.psum_scatter(partial, 'dp', scatter_dimension=0, tiled=True)[0]  148 us
    all_gather x1, waiting for transfers between devices, per_device(): lax.all_gather(jnp.concatenate([gate_grad, up_grad], axis=1), 'dp', axis=0)  106 us
    reduce_scatter x1, waiting for transfers between devices, per_device(): lax.psum_scatter(parts, 'tensor', scatter_dimension=0, tiled=True)[0]  52.9 us
    all_gather x1, waiting for transfers between devices, per_device(): toks = lax.all_gather(mine, 'tensor', axis=0)  37.9 us
    all_to_all x1, blocking collectives, per_device(): mine = lax.all_to_all(spread, 'dp', 0, 0, tiled=True)  29.9 us
    all_to_all x1, blocking collectives, per_device(): back = lax.all_to_all(summed, 'dp', 0, 0, tiled=True)  27.2 us
    pallas_call x1, Pallas kernels, per_device(): pl.pallas_call(backward_kernel, grid_spec=pltpu.PrefetchScalarGridSpec(nu...  27 us
    pallas_call x1, Pallas kernels, per_device(): pl.pallas_call(forward_kernel, grid_spec=pltpu.PrefetchScalarGridSpec(num...  16 us
  transfers between devices with their start and end apart: 4, of which 4 were waited for; matrix products, arithmetic and copies ran while one was open for 0% of the time, Pallas kernels for 0%

profile of v1, /device:TPU:7, one launch (start us, length us, event | category | flops | bytes accessed | tf_op | source)
XLA Modules:
  0.0 503.0 jit_solution(16867223722344988260)
XLA Ops:
  7.2 0.0 copy-start.6
  7.2 0.0 copy-start.5
  7.2 0.0 copy-start.1
  7.2 0.0 all-gather.6.cloned.1.call-start
  7.2 13.5 %all_to_all.20 = bf16[8,32,1024]{2,1,0:T(8,128)(2,1)S(1)} all-to-all(bf16[8,32,1024]{2,1,0:T(8,128)(2,1)} %bitcast.31), channel_id=1, replica_groups=mesh['dp'=32,'tensor'=8] {'tensor'}, dimensions={0} | all-to-all | bytes 1048576 | tf_op jit(solution)/shard_map/all_to_all | solution.py:69
  20.7 0.1 fusion.7
  20.8 29.9 %all_to_all.21 = bf16[32,32,256]{2,1,0:T(8,128)(2,1)} all-to-all(bf16[32,32,256]{2,1,0:T(8,128)(2,1)S(1)} %bitcast.27), channel_id=1, replica_groups=mesh['dp'=32,'tensor'=8] {'dp'}, dimensions={0} | all-to-all | bytes 1048576 | tf_op jit(solution)/shard_map/all_to_all | solution.py:71
  50.7 0.0 all-gather.6.cloned.1.call-update
  50.7 0.0 reduce-scatter.3.cloned.1.call-start
  50.8 0.0 copy-done.6
  50.8 0.6 dynamic-slice
  52.0 0.0 copy-done.5
  52.1 0.1 bitcast_dynamic-update-slice_fusion
  52.2 10.5 %all-reduce.listed = s32[64]{0:T(128)S(1)} all-reduce(s32[64]{0:T(128)S(1)} %bitcast_dynamic-update-slice_fusion), channel_id=2, replica_groups=mesh['dp'=32,'tensor'=8] {'dp'}, use_global_device_ids=true, to_apply=%add | all-reduce | flops 64 | bytes 512 | tf_op jit(solution)/shard_map/all_gather | solution.py:67
  62.7 37.9 %all-gather.6.cloned.1.call-done = bf16[256,32,256]{2,1,0:T(8,128)(2,1)} async-done(((bf16[32,32,256]{2,1,0:T(8,128)(2,1)}), bf16[256,32,256]{2,1,0:T(8,128)(2,1)}) %all-gather.6.cloned.1.call-update) | async-done | bytes 4194320 | tf_op jit(solution)/shard_map/all_gather | solution.py:72
  100.6 0.0 copy-done.1
  100.6 0.0 copy-start
  100.6 2.2 copy-done
  102.8 0.0 copy-start.2
  102.8 1.5 copy-done.2
  104.3 16.0 %shard_map.76 = bf16[32,256,512]{2,1,0:T(8,128)(2,1)} custom-call(s32[64]{0:T(128)S(1)} %all-reduce.listed, bf16[8,32,32,256]{3,2,1,0:T(8,128)(2,1)S(1)} %bitcast.25, bf16[256,3584]{1,0:T(8,128)(2,1)S(1)} %copy-done.1, bf16[256,3584]{1,0:T(8,128)(2,1)S(1)} %copy-done.2), custom_call_target="tpu_custom_call" | custom-call | tf_op jit(solution)/shard_map/pallas_call | solution.py:77
  120.3 0.0 copy-start.4
  120.3 0.0 reduce-scatter.3.cloned.1.call-update
  120.4 0.0 all-gather.8.cloned.1.call-start
  120.4 0.1 broadcast_bitcast_fusion
  120.5 147.8 %reduce-scatter.3.cloned.1.call-done = bf16[1,256,512]{2,1,0:T(8,128)(2,1)} async-done(((bf16[32,256,512]{2,1,0:T(8,128)(2,1)}), bf16[1,256,512]{2,1,0:T(8,128)(2,1)}) %reduce-scatter.3.cloned.1.call-update) | async-done | bytes 262160 | tf_op jit(solution)/shard_map/reduce_scatter | solution.py:85
  268.2 1.0 bitcast_convert_fusion
  269.2 0.0 copy-done.4
  269.3 0.1 fusion.3
  269.4 0.7 pad_maximum_fusion.1
  270.1 0.0 all-gather.8.cloned.1.call-update
  270.1 0.0 reduce-scatter.5.cloned.1.call-start
  270.1 105.9 %all-gather.8.cloned.1.call-done = bf16[8192,512]{1,0:T(8,128)(2,1)} async-done(((bf16[256,512]{1,0:T(8,128)(2,1)}), bf16[8192,512]{1,0:T(8,128)(2,1)}) %all-gather.8.cloned.1.call-update) | async-done | bytes 8388624 | tf_op jit(solution)/shard_map/all_gather | solution.py:94
  376.0 0.0 copy-start.3
  376.0 1.5 copy-done.3
  377.5 27.0 %shard_map.77 = (bf16[8,32,32,256]{3,2,1,0:T(8,128)(2,1)}, bf16[256,3584]{1,0:T(8,128)(2,1)}, bf16[256,3584]{1,0:T(8,128)(2,1)}) custom-call(s32[64]{0:T(128)S(1)} %all-reduce.listed, bf16[8,32,32,256]{3,2,1,0:T(8,128)(2,1)} %bitcast.24, bf16[32,256,512]{2,1,0:T(8,128)(2,1)} %bitcast.26, bf16[256,3584]{1,0:T(8,128)(2,1)S(1)} %copy-done.1, ...), custom_call_target="tpu_custom_call" | custom-call | tf_op jit(solution)/shard_map/pallas_call | solution.py:96
  404.6 0.0 reduce-scatter.5.cloned.1.call-update
  404.6 52.9 %reduce-scatter.5.cloned.1.call-done = bf16[1,32,32,256]{3,2,1,0:T(8,128)(2,1)} async-done(((bf16[8,32,32,256]{3,2,1,0:T(8,128)(2,1)}), bf16[1,32,32,256]{3,2,1,0:T(8,128)(2,1)}) %reduce-scatter.5.cloned.1.call-update) | async-done | bytes 524304 | tf_op jit(solution)/shard_map/reduce_scatter | solution.py:112
  457.5 27.2 %all_to_all.22 = bf16[32,32,256]{2,1,0:T(8,128)(2,1)S(1)} all-to-all(bf16[32,32,256]{2,1,0:T(8,128)(2,1)} %bitcast.32), channel_id=1, replica_groups=mesh['dp'=32,'tensor'=8] {'dp'}, dimensions={0} | all-to-all | bytes 1048576 | tf_op jit(solution)/shard_map/all_to_all | solution.py:113
  484.7 0.4 copy.11
  485.1 0.4 reshape.50
  485.5 10.2 %all_to_all.23 = bf16[8,32,1024]{2,1,0:T(8,128)(2,1)S(1)} all-to-all(bf16[8,32,1024]{2,1,0:T(8,128)(2,1)S(1)} %reshape.50), channel_id=1, replica_groups=mesh['dp'=32,'tensor'=8] {'tensor'}, dimensions={0} | all-to-all | bytes 1048576 | tf_op jit(solution)/shard_map/all_to_all | solution.py:115
  495.7 0.8 copy.14
  (3 shorter events, 0.0 us)
Async XLA Ops:
  7.2 43.6 %copy-start.6 = (u32[256]{0:T(256)S(1)}, u32[256]{0:T(256)}, u32[]{:S(2)}) copy-start(u32[256]{0:T(256)} %constant.10) | copy-start | bytes 3076
  7.2 44.9 %copy-start.5 = (s32[1,1,2]{2,1,0:T(1,128)S(1)}, s32[1,1,2]{2,1,0:T(1,128)}, u32[]{:S(2)}) copy-start(s32[1,1,2]{2,1,0:T(1,128)} %param.7) | copy-start | bytes 28
  7.2 93.4 %copy-start.1 = (bf16[256,3584]{1,0:T(8,128)(2,1)S(1)}, bf16[256,3584]{1,0:T(8,128)(2,1)}, u32[]{:S(2)}) copy-start(bf16[256,3584]{1,0:T(8,128)(2,1)} %gate_ref.3) | copy-start | bytes 5505028
  7.2 93.4 %all-gather.6.cloned.1.call-start = ((), (), s32[]{:S(2)}) async-start(), calls=%async_computation.8 | async-start | bytes 4718592 | tf_op jit(solution)/shard_map/all_gather | solution.py:72
  50.7 217.5 %reduce-scatter.3.cloned.1.call-start = ((), (), s32[]{:S(2)}) async-start(), calls=%async_computation.6 | async-start | bytes 8650752 | tf_op jit(solution)/shard_map/reduce_scatter | solution.py:85
  100.6 2.2 copy-start
  102.8 1.5 copy-start.2
  120.3 148.9 %copy-start.4 = (bf16[256,1,256]{2,0,1:T(8,128)(2,1)S(1)}, bf16[256,1,256]{2,0,1:T(8,128)(2,1)}, u32[]{:S(2)}) copy-start(bf16[256,1,256]{2,0,1:T(8,128)(2,1)} %param.6) | copy-start | bytes 393220
  120.4 255.7 %all-gather.8.cloned.1.call-start = ((), (), s32[]{:S(2)}) async-start(), calls=%async_computation.9 | async-start | bytes 8650752 | tf_op jit(solution)/shard_map/all_gather | solution.py:94
  270.1 187.4 %reduce-scatter.5.cloned.1.call-start = ((), (), s32[]{:S(2)}) async-start(), calls=%async_computation.7 | async-start | bytes 4718592 | tf_op jit(solution)/shard_map/reduce_scatter | solution.py:112
  376.0 1.5 copy-start.3
Sparse Core Ops, SparseCore 0:
  50.8 49.7 all-gather.5
  120.5 147.7 reduce-scatter.2
  271.6 104.3 all-gather.7
  404.7 52.7 reduce-scatter.4

commit v2 on v1

v2 whole, which is shorter than its diff:
```python
import jax
import jax.numpy as jnp
from jax import lax
from jax.experimental import pallas as pl
from jax.experimental.pallas import tpu as pltpu
from jax.sharding import PartitionSpec as P

MESH = pl.DeviceIdType.MESH
BLOCK, TILE, CAP = 128, 256, 2
NZ, QUARTERS, TENSOR, DP = 8, 4, 8, 32
ROWS = 256
SHARE = TILE // TENSOR
UNITS = 2 * CAP * BLOCK
BF16, F32 = jnp.bfloat16, jnp.float32


def send(src, dst, send_sem, recv_sem, device):
    pltpu.make_async_remote_copy(
        src_ref=src, dst_ref=dst, send_sem=send_sem, recv_sem=recv_sem, device_id=device, device_id_type=MESH
    ).start()


def wait(ref, sem):
    pltpu.make_async_copy(ref, ref, sem).wait()


def main_kernel(
    tokens, live_grad, act, wg_hbm, wu_hbm,
    out, pieces_hbm, listed,
    wg, wu, listed_v, tok, sc, rc, sz, rz, xs, xr, acc, gr, part, piece, yr1, yr2, xr2, fin,
    s_t1, r_t1, s_act, r_act, l_act, s_w, s_x, r_x, s_y, r_y, s_f, r_f, s_c, r_c, s_z, r_z, s_h, r_h,
    s_gh, r_gh, s_gz, r_gz, s_gc, r_gc, s_0, r_0, s_1, r_1, s_2, r_2, s_o, r_o, s_p,
):
    d, t = lax.axis_index("dp"), lax.axis_index("tensor")
    z, a = d // QUARTERS, lax.rem(d, QUARTERS)
    xh, c = a // 2, lax.rem(a, 2)
    xl, y = t // 4, lax.rem(t, 4)
    at_home = t == z

    def plane(dz):
        return lax.rem(z + dz + NZ, NZ)

    up_z, down_z = (plane(1) * 4 + a, t), (plane(-1) * 4 + a, t)
    sibling = (d + 1 - 2 * c, t)
    across = (z * 4 + (1 - xh) * 2 + c, t)
    beside = (d, (1 - xl) * 4 + y)
    y_next, y_last, y_far = lax.rem(y + 1, 4), lax.rem(y + 3, 4), lax.rem(y + 2, 4)
    up_y, down_y = (d, xl * 4 + y_next), (d, xl * 4 + y_last)

    def load_block(b, _):
        columns = pl.ds(pl.multiple_of(b * BLOCK, BLOCK), BLOCK)
        pltpu.make_async_copy(wg_hbm.at[:, columns], wg.at[b], s_w.at[0]).start()
        pltpu.make_async_copy(wu_hbm.at[:, columns], wu.at[b], s_w.at[1]).start()
        return 0

    lax.fori_loop(0, wg.shape[0], load_block, 0)

    barrier = pltpu.get_barrier_semaphore()

    def greet(device):
        pl.semaphore_signal(barrier, inc=1, device_id=device, device_id_type=MESH)

    def spread_to(k):
        return (t * QUARTERS + k // TENSOR, lax.rem(k, TENSOR))

    def greet_all(k, _):
        other = spread_to(k)
        mine = jnp.logical_and(other[0] == d, other[1] == t)

        @pl.when(jnp.logical_not(mine))
        def _():
            greet(other)

        source_is_me = jnp.logical_and(k == d, at_home)

        @pl.when(jnp.logical_not(source_is_me))
        def _():
            greet((k, z))

        return 0

    lax.fori_loop(0, DP, greet_all, 0)

    def greet_dp(k, _):
        greet((lax.rem(d + k, DP), t))
        return 0

    lax.fori_loop(1, DP, greet_dp, 0)
    for device in (beside, up_y, down_y):
        greet(device)
    pl.semaphore_wait(barrier, DP + DP - 1 + DP + 3 - jnp.where(at_home, 2, 0))

    def spread(k, _):
        other = spread_to(k)
        quarter, share = k // TENSOR, lax.rem(k, TENSOR)
        src = tokens.at[pl.ds(pl.multiple_of(share * SHARE, SHARE), SHARE), pl.ds(pl.multiple_of(quarter * ROWS, ROWS), ROWS)]
        dst = tok.at[share // 4, lax.rem(share, 4), d]
        mine = jnp.logical_and(other[0] == d, other[1] == t)

        @pl.when(jnp.logical_not(mine))
        def _():
            send(src, dst, s_t1, r_t1.at[z], other)

        @pl.when(mine)
        def _():
            pltpu.make_async_copy(src, dst, r_t1.at[z]).start()

        return 0

    lax.fori_loop(0, DP, spread, 0)

    own_row = pltpu.make_async_copy(act, listed_v.at[d], l_act)
    own_row.start()

    def tell(k, _):
        send(act, listed_v.at[d], s_act, r_act, (lax.rem(d + k, DP), t))
        return 0

    lax.fori_loop(1, DP, tell, 0)

    order = [plane(k) for k in (4, 3, -3, 2, -2, 1, -1, 0)]

    def four(zq):
        return pl.ds(zq * 4, 4)

    def stage_x(o):
        mine = tok.at[xl, y, four(order[o])]
        wait(mine, r_t1.at[order[o]])
        send(mine, mine, s_x, r_x.at[o], beside)

    def stage_y(o):
        wait(tok.at[1 - xl, y, four(order[o])], r_x.at[o])
        both = tok.at[:, y, four(order[o])]
        send(both, both, s_y, r_y.at[0, o], up_y)
        send(both, both, s_y, r_y.at[1, o], down_y)

    def stage_f(o):
        first, second = pl.ds(order[o] * 4, 2), pl.ds(order[o] * 4 + 2, 2)
        wait(tok.at[:, y_last, four(order[o])], r_y.at[0, o])
        send(tok.at[:, y_last, first], tok.at[:, y_last, first], s_f, r_f.at[0, o], up_y)
        wait(tok.at[:, y_next, four(order[o])], r_y.at[1, o])
        send(tok.at[:, y_next, second], tok.at[:, y_next, second], s_f, r_f.at[1, o], down_y)

    def tile_weights(q):
        picked = [listed[q, 0, k] for k in range(CAP)]
        return jnp.concatenate([ref[b] for ref in (wg, wu) for b in picked], axis=1)

    def tile_tokens(q):
        return tok[:, :, q].reshape(TILE, ROWS)

    def partial_sum(q):
        return jnp.dot(tile_tokens(q), tile_weights(q), preferred_element_type=F32)

    def settle(o, k, received):
        total = partial_sum(order[o] * 4 + k * 2 + c)
        wait(rc.at[o, k], r_c.at[o, k])
        total = total + rc[o, k].astype(F32)
        for slot in received:
            wait(rz.at[slot, k], r_z.at[slot, k])
            total = total + rz[slot, k].astype(F32)
        return total

    def stage_c(o):
        wait(tok.at[:, y_far, pl.ds(order[o] * 4, 2)], r_f.at[0, o])
        wait(tok.at[:, y_far, pl.ds(order[o] * 4 + 2, 2)], r_f.at[1, o])

        def for_sibling(k, _):
            sc[o, k] = partial_sum(order[o] * 4 + k * 2 + 1 - c).astype(BF16)
            send(sc.at[o, k], rc.at[o, k], s_c, r_c.at[o, k], sibling)
            return 0

        lax.fori_loop(0, 2, for_sibling, 0)
        if o == 0:
            for k, slot, device in ((0, 0, up_z), (1, 1, down_z)):
                sz[o, k] = settle(o, k, ()).astype(BF16)
                send(sz.at[o, k], rz.at[slot, k], s_z, r_z.at[slot, k], device)
        elif o <= 2:
            device = up_z if o == 1 else down_z
            for k in (o - 1, 2 - o):
                sz[o, k] = settle(o, k, (o - 1,) if k == o - 1 else ()).astype(BF16)
                send(sz.at[o, k], rz.at[o + 1, k], s_z, r_z.at[o + 1, k], device)
        elif o <= 6:
            device = up_z if o % 2 else down_z

            def along(k, _):
                sz[o, k] = settle(o, k, (o - 1,)).astype(BF16)
                send(sz.at[o, k], rz.at[o + 1, k], s_z, r_z.at[o + 1, k], device)
                return 0

            lax.fori_loop(0, 2, along, 0)
        else:
            xs[...] = settle(o, 1 - xh, (6, 7)).astype(BF16)
            send(xs, xr, s_h, r_h, across)
            acc[...] = settle(o, xh, (6, 7))

    for o in range(NZ):
        stage_x(o)
        if o == 0:
            wait(wg, s_w.at[0])
            wait(wu, s_w.at[1])
            own_row.wait()
            wait(listed_v.at[pl.ds(0, DP - 1)], r_act)
            to_smem = pltpu.make_async_copy(listed_v, listed, l_act)
            to_smem.start()
            to_smem.wait()
    for o in range(3):
        stage_y(o)
    stage_f(0)
    for o in range(NZ):
        if o + 3 < NZ:
            stage_y(o + 3)
        if o + 1 < NZ:
            stage_f(o + 1)
        stage_c(o)

    wait(xr, r_h)
    both = acc[...] + xr[...].astype(F32)
    gate, up = both[:, : CAP * BLOCK], both[:, CAP * BLOCK :]
    g = live_grad[...].astype(F32)
    relu = jnp.maximum(gate, 0.0)
    gr[d, :, : CAP * BLOCK] = (g * up * 2.0 * relu).astype(BF16)
    gr[d, :, CAP * BLOCK :] = (g * relu * relu).astype(BF16)

    def own(zq, k):
        return gr.at[zq * 4 + k * 2 + c]

    def pass_on(zq, k, direction, distance):
        tile = own(zq, k)
        send(tile, tile, s_gz, r_gz.at[direction, distance, k], up_z if direction == 0 else down_z)

    def to_sibling(e, zq, k):
        tile = own(zq, k)
        send(tile, tile, s_gc, r_gc.at[e, k], sibling)

    send(gr.at[d], gr.at[d], s_gh, r_gh, across)
    pass_on(z, xh, 0, 0)
    pass_on(z, xh, 1, 0)
    to_sibling(0, z, xh)
    wait(own(z, 1 - xh), r_gh)
    pass_on(z, 1 - xh, 0, 0)
    pass_on(z, 1 - xh, 1, 0)
    to_sibling(0, z, 1 - xh)

    arrivals = [plane(k) for k in (0, -1, 1, -2, 2, -3, 3, 4)]

    def arrive(distance):
        for k in (0, 1):
            for direction in (0, 1):
                e = 1 + 2 * distance + direction
                zq = arrivals[e]
                wait(own(zq, k), r_gz.at[direction, distance, k])
                if distance < 2 or k == direction:
                    pass_on(zq, k, direction, distance + 1)
                to_sibling(e, zq, k)

    def arrive_last():
        for k in (0, 1):
            wait(own(arrivals[7], k), r_gz.at[k, 3, k])
            to_sibling(7, arrivals[7], k)

    def backward(e):
        zq = arrivals[e]
        for k in (0, 1):
            wait(gr.at[zq * 4 + k * 2 + 1 - c], r_gc.at[e, k])

        def one(k, _):
            q = zq * 4 + k
            grads = gr[q]
            value = lax.dot_general(grads, tile_weights(q), (((1,), (1,)), ((), ())), preferred_element_type=F32)
            part[:, :, q] = value.astype(BF16).reshape(2, 4, SHARE, ROWS)
            value = lax.dot_general(tile_tokens(q), grads, (((0,), (0,)), ((), ())), preferred_element_type=F32)
            piece[q] = value.astype(BF16)
            return 0

        lax.fori_loop(0, 4, one, 0)
        pltpu.make_async_copy(piece.at[four(zq)], pieces_hbm.at[four(zq)], s_p).start()
        first, second = pl.ds(zq * 4, 2), pl.ds(zq * 4 + 2, 2)
        send(part.at[:, y_far, first], yr1.at[0, e], s_0, r_0.at[0, e], up_y)
        send(part.at[:, y_far, second], yr1.at[1, e], s_0, r_0.at[1, e], down_y)

    def reduce_1(e):
        zq = arrivals[e]
        for direction, y_to, device in ((0, y_next, up_y), (1, y_last, down_y)):
            wait(yr1.at[direction, e], r_0.at[direction, e])
            half = pl.ds(zq * 4 + 2 * direction, 2)
            part[:, y_to, half] = (part[:, y_to, half].astype(F32) + yr1[direction, e].astype(F32)).astype(BF16)
            send(part.at[:, y_to, four(zq)], yr2.at[direction, e], s_1, r_1.at[direction, e], device)

    def reduce_2(e):
        zq = arrivals[e]
        for direction in (0, 1):
            wait(yr2.at[direction, e], r_1.at[direction, e])
        total = part[:, y, four(zq)].astype(F32) + yr2[0, e].astype(F32) + yr2[1, e].astype(F32)
        part[:, y, four(zq)] = total.astype(BF16)
        send(part.at[1 - xl, y, four(zq)], xr2.at[e], s_2, r_2.at[e], beside)

    def reduce_3(e):
        zq = arrivals[e]
        wait(xr2.at[e], r_2.at[e])
        fin[four(zq)] = (part[xl, y, four(zq)].astype(F32) + xr2[e].astype(F32)).astype(BF16)

        def home(k, _):
            q = zq * 4 + k
            dst = out.at[pl.ds(pl.multiple_of(t * SHARE, SHARE), SHARE), pl.ds(pl.multiple_of(a * ROWS, ROWS), ROWS)]
            mine = jnp.logical_and(q == d, at_home)

            @pl.when(jnp.logical_not(mine))
            def _():
                send(fin.at[q], dst, s_o, r_o, (q, z))

            @pl.when(mine)
            def _():
                pltpu.make_async_copy(fin.at[q], dst, r_o).start()

            return 0

        lax.fori_loop(0, 4, home, 0)

    for e in range(NZ + 3):
        if e == 1 or e == 3 or e == 5:
            arrive(e // 2)
        if e == 7:
            arrive_last()
        if e < NZ:
            backward(e)
        if 0 <= e - 1 < NZ:
            reduce_1(e - 1)
        if 0 <= e - 2 < NZ:
            reduce_2(e - 2)
        if 0 <= e - 3 < NZ:
            reduce_3(e - 3)

    wait(out, r_o)

    for sem in (s_t1, s_o):

        @pl.when(at_home)
        def _():
            wait(fin.at[pl.ds(0, DP - 1)], sem)

        @pl.when(jnp.logical_not(at_home))
        def _():
            wait(fin, sem)

    wait(listed_v.at[pl.ds(0, DP - 1)], s_act)
    wait(fin, s_x)
    wait(tok.at[0], s_y)
    wait(tok.at[0, pl.ds(0, 2)], s_f)
    wait(sc, s_c)
    wait(sz, s_z)
    wait(xs, s_h)
    wait(gr.at[d], s_gh)
    wait(gr.at[pl.ds(0, 14)], s_gz)
    wait(gr.at[pl.ds(0, 16)], s_gc)
    wait(yr1, s_0)
    wait(yr2, s_1)
    wait(xr2, s_2)
    wait(piece, s_p)


def sum_kernel(listed, piece_ref, dgate_ref, dup_ref, gate_acc, up_acc):
    step = pl.program_id(0)
    tiles = piece_ref.shape[0]

    @pl.when(step == 0)
    def _():
        gate_acc[...] = jnp.zeros_like(gate_acc)
        up_acc[...] = jnp.zeros_like(up_acc)

    for k in range(tiles):
        for c in range(CAP):
            block = listed[step * tiles + k, 0, c]
            at = pl.ds(pl.multiple_of(block * BLOCK, BLOCK), BLOCK)
            for m, acc in enumerate((gate_acc, up_acc)):
                column = (m * CAP + c) * BLOCK
                acc[:, at] += piece_ref[k, :, column : column + BLOCK].astype(F32)

    @pl.when(step == pl.num_programs(0) - 1)
    def _():
        dgate_ref[...] = gate_acc[...].astype(BF16)
        dup_ref[...] = up_acc[...].astype(BF16)


def per_device(tokens, out_grad, active, w_gate, w_up):
    width = w_gate.shape[1]
    blocks = width // BLOCK
    act = jnp.pad(jnp.minimum(active.reshape(1, CAP), blocks - 1), ((0, 0), (0, BLOCK - CAP)))
    live = jnp.repeat(active.reshape(1, CAP) < blocks, BLOCK, axis=1)
    live_grad = jnp.where(live, out_grad.reshape(TILE, CAP * BLOCK), 0)
    vmem = pl.BlockSpec(memory_space=pltpu.VMEM)
    anywhere = pl.BlockSpec(memory_space=pl.ANY)
    dma, v = pltpu.SemaphoreType.DMA, pltpu.VMEM
    tile = (TILE, UNITS)
    slab = (SHARE, ROWS)
    input_grad, pieces, listed = pl.pallas_call(
        main_kernel,
        in_specs=[vmem, vmem, vmem, anywhere, anywhere],
        out_specs=[vmem, anywhere, pl.BlockSpec(memory_space=pltpu.SMEM)],
        out_shape=[
            jax.ShapeDtypeStruct((TILE, QUARTERS * ROWS), BF16),
            jax.ShapeDtypeStruct((DP, ROWS, UNITS), BF16),
            jax.ShapeDtypeStruct((DP, 1, BLOCK), jnp.int32),
        ],
        scratch_shapes=[
            v((blocks, ROWS, BLOCK), BF16),
            v((blocks, ROWS, BLOCK), BF16),
            v((DP, 1, BLOCK), jnp.int32),
            v((2, 4, DP, *slab), BF16),
            v((NZ, 2, *tile), BF16),
            v((NZ, 2, *tile), BF16),
            v((NZ - 1, 2, *tile), BF16),
            v((NZ, 2, *tile), BF16),
            v(tile, BF16),
            v(tile, BF16),
            v(tile, F32),
            v((DP, *tile), BF16),
            v((2, 4, DP, *slab), BF16),
            v((DP, ROWS, UNITS), BF16),
            v((2, NZ, 2, 2, *slab), BF16),
            v((2, NZ, 2, 4, *slab), BF16),
            v((NZ, 4, *slab), BF16),
            v((DP, *slab), BF16),
            dma, dma((NZ,)), dma, dma, dma, dma((2,)),
            dma, dma((NZ,)), dma, dma((2, NZ)), dma, dma((2, NZ)),
            dma, dma((NZ, 2)), dma, dma((NZ, 2)), dma, dma,
            dma, dma, dma, dma((2, 4, 2)), dma, dma((NZ, 2)),
            dma, dma((2, NZ)), dma, dma((2, NZ)), dma, dma((NZ,)),
            dma, dma, dma,
        ],
        compiler_params=pltpu.CompilerParams(
            collective_id=0, has_side_effects=True, vmem_limit_bytes=62 * 2**20
        ),
    )(tokens, live_grad, act, w_gate, w_up)

    tiles = 4
    whole = pl.BlockSpec((ROWS, width), lambda q, *_: (0, 0))
    dgate, dup = pl.pallas_call(
        sum_kernel,
        grid_spec=pltpu.PrefetchScalarGridSpec(
            num_scalar_prefetch=1,
            grid=(DP // tiles,),
            in_specs=[pl.BlockSpec((tiles, ROWS, UNITS), lambda q, *_: (q, 0, 0))],
            out_specs=[whole, whole],
            scratch_shapes=[v((ROWS, width), F32)] * 2,
        ),
        out_shape=[jax.ShapeDtypeStruct((ROWS, width), BF16)] * 2,
        compiler_params=pltpu.CompilerParams(vmem_limit_bytes=40 * 2**20),
    )(listed, pieces)
    return input_grad, dgate, dup


def solution(mesh):
    placed = (
        P("dp", "tensor"),
        P("dp", "tensor", None),
        P("dp", "tensor", None),
        P("dp", "tensor"),
        P("dp", "tensor"),
    )
    return jax.shard_map(
        per_device,
        mesh=mesh,
        in_specs=placed,
        out_specs=(P("dp", "tensor"), P("dp", "tensor"), P("dp", "tensor")),
        check_vma=False,
    )
```

time: 507 us -> 235 us (0.46)
  waiting for transfers between devices: 345 us -> 0 us
  Pallas kernels: 43.1 us -> 226 us
  blocking collectives: 91.3 us -> 0 us
  between operations: 14.5 us -> 0.65 us
    reduce_scatter x2 -> x0, waiting for transfers between devices: 201 us -> none  [the longest x1 148 us: per_device(): lax.psum_scatter(partial, 'dp', scatter_dimension=0, tiled=True)[0]]
    pallas_call x2, Pallas kernels: 43.1 us -> 226 us  [the longest x1 219 us: per_device(): pl.pallas_call(main_kernel, in_specs=[vmem, vmem, vmem, anywhere, anywher...]
    all_gather x2 -> x0, waiting for transfers between devices: 144 us -> none  [the longest x1 106 us: per_device(): lax.all_gather(jnp.concatenate([gate_grad, up_grad], axis=1), 'dp', axis=0)]
    all_to_all x4 -> x0, blocking collectives: 80.7 us -> none  [the longest x1 29.9 us: per_device(): mine = lax.all_to_all(spread, 'dp', 0, 0, tiled=True)]
    all_gather x1 -> x0, blocking collectives: 10.5 us -> none  [per_device(): listed = lax.all_gather(active.reshape(CAP), 'dp', axis=0, tiled=True)]
  transfers between devices with their start and end apart: 4 -> 0, of which waited for: 4 -> 0; matrix products, arithmetic and copies ran while one was open for 0% -> 0% of each run, Pallas kernels for 0% -> 0%
where the time goes in v2:
time: 235 us
  Pallas kernels  226 us (96%)
  local copies, waits for them, and re-layouts  5.48 us (2%)
  other arithmetic  2.89 us (1%)
    pallas_call x1, Pallas kernels, per_device(): pl.pallas_call(main_kernel, in_specs=[vmem, vmem, vmem, anywhere, anywher...  219 us
    pallas_call x1, Pallas kernels, per_device(): pl.pallas_call(sum_kernel, grid_spec=pltpu.PrefetchScalarGridSpec(num_sca...  6.66 us
    unnamed x7, local copies, waits for them, and re-layouts  4.89 us

profile of v2, /device:TPU:7, one launch (start us, length us, event | category | flops | bytes accessed | tf_op | source)
XLA Modules:
  0.0 234.9 jit_solution(4371670432598399649)
XLA Ops:
  0.6 0.7 minimum_bitcast_fusion
  1.3 0.5 pad.4.act
  1.8 0.7 compare_bitcast_fusion
  2.5 0.1 broadcast_bitcast_fusion
  2.5 1.6 bitcast_select_fusion.live_grad
  4.1 219.2 %shard_map.76 = (bf16[256,1024]{1,0:T(8,128)(2,1)}, bf16[32,256,512]{2,1,0:T(8,128)(2,1)}, s32[32,1,128]{2,1,0:T(1,128)}) custom-call(bf16[256,1024]{1,0:T(8,128)(2,1)} %tokens.1, bf16[256,256]{1,0:T(8,128)(2,1)} %bitcast_select_fusion.live_grad, s32[1,128]{1,0:T(1,128)} %pad.4.act, bf16[256,3584]{1,0:T(8,128)(2,1)} %wg_hbm.1, bf16[256,3584]{1,0:T(8,128)(2,1)} %wu_hbm.1), custom_call_target="tpu_custom_call" | custom-call | tf_op jit(solution)/shard_map/pallas_call | solution.py:395
  223.4 0.0 copy-start
  223.4 3.4 %copy-done = bf16[32,256,512]{2,1,0:T(8,128)(2,1)S(1)} copy-done((bf16[32,256,512]{2,1,0:T(8,128)(2,1)S(1)}, bf16[32,256,512]{2,1,0:T(8,128)(2,1)}, u32[]{:S(2)}) %copy-start) | copy-done | bytes 8388632
  226.8 0.0 copy-start.1
  226.8 0.7 copy-done.1
  227.5 0.0 copy-start.2
  227.5 6.7 %shard_map.77 = (bf16[256,3584]{1,0:T(8,128)(2,1)}, bf16[256,3584]{1,0:T(8,128)(2,1)}) custom-call(s32[32,1,128]{2,1,0:T(1,128)S(1)} %copy-done.1, bf16[32,256,512]{2,1,0:T(8,128)(2,1)S(1)} %copy-done), custom_call_target="tpu_custom_call" | custom-call | tf_op jit(solution)/shard_map/pallas_call | solution.py:437
  234.1 0.0 copy-done.2
  234.1 0.8 copy.9
Async XLA Ops:
  223.4 3.4 %copy-start = (bf16[32,256,512]{2,1,0:T(8,128)(2,1)S(1)}, bf16[32,256,512]{2,1,0:T(8,128)(2,1)}, u32[]{:S(2)}) copy-start(bf16[32,256,512]{2,1,0:T(8,128)(2,1)} %get-tuple-element.10.piece_ref) | copy-start | bytes 25165828
  226.8 0.7 copy-start.1
  227.5 6.7 %copy-start.2 = (bf16[256,1024]{1,0:T(8,128)(2,1)S(1)}, bf16[256,1024]{1,0:T(8,128)(2,1)}, u32[]{:S(2)}) copy-start(bf16[256,1024]{1,0:T(8,128)(2,1)} %get-tuple-element.16) | copy-start | bytes 1572868

commit v3 on v2

--- a/solution.py
+++ b/solution.py
@@ -25,17 +25,16 @@
 
 
 def main_kernel(
-    tokens, live_grad, act, wg_hbm, wu_hbm,
+    tokens, out_grad, live, act, wg_hbm, wu_hbm,
     out, pieces_hbm, listed,
-    wg, wu, listed_v, tok, sc, rc, sz, rz, xs, xr, acc, gr, part, piece, yr1, yr2, xr2, fin,
+    wg, wu, listed_v, tok, sc, rc, sz, rz, xs, xr, acc, gr, part, piece, yr1, yr2, xr2, fin, ts, back,
     s_t1, r_t1, s_act, r_act, l_act, s_w, s_x, r_x, s_y, r_y, s_f, r_f, s_c, r_c, s_z, r_z, s_h, r_h,
-    s_gh, r_gh, s_gz, r_gz, s_gc, r_gc, s_0, r_0, s_1, r_1, s_2, r_2, s_o, r_o, s_p,
+    s_gh, r_gh, s_gz, r_gz, s_gc, r_gc, s_0, r_0, s_1, r_1, s_2, r_2, s_o, r_o, s_p, s_ts, r_ts, s_out, r_out,
 ):
     d, t = lax.axis_index("dp"), lax.axis_index("tensor")
     z, a = d // QUARTERS, lax.rem(d, QUARTERS)
     xh, c = a // 2, lax.rem(a, 2)
     xl, y = t // 4, lax.rem(t, 4)
-    at_home = t == z
 
     def plane(dz):
         return lax.rem(z + dz + NZ, NZ)
@@ -60,54 +59,28 @@
     def greet(device):
         pl.semaphore_signal(barrier, inc=1, device_id=device, device_id_type=MESH)
 
-    def spread_to(k):
-        return (t * QUARTERS + k // TENSOR, lax.rem(k, TENSOR))
-
-    def greet_all(k, _):
-        other = spread_to(k)
-        mine = jnp.logical_and(other[0] == d, other[1] == t)
-
-        @pl.when(jnp.logical_not(mine))
-        def _():
-            greet(other)
-
-        source_is_me = jnp.logical_and(k == d, at_home)
-
-        @pl.when(jnp.logical_not(source_is_me))
-        def _():
-            greet((k, z))
-
-        return 0
-
-    lax.fori_loop(0, DP, greet_all, 0)
-
     def greet_dp(k, _):
         greet((lax.rem(d + k, DP), t))
         return 0
 
+    def greet_plane(k, _):
+        greet((d, lax.rem(t + k, TENSOR)))
+        return 0
+
+    lax.fori_loop(1, TENSOR, greet_plane, 0)
     lax.fori_loop(1, DP, greet_dp, 0)
-    for device in (beside, up_y, down_y):
-        greet(device)
-    pl.semaphore_wait(barrier, DP + DP - 1 + DP + 3 - jnp.where(at_home, 2, 0))
-
-    def spread(k, _):
-        other = spread_to(k)
-        quarter, share = k // TENSOR, lax.rem(k, TENSOR)
-        src = tokens.at[pl.ds(pl.multiple_of(share * SHARE, SHARE), SHARE), pl.ds(pl.multiple_of(quarter * ROWS, ROWS), ROWS)]
-        dst = tok.at[share // 4, lax.rem(share, 4), d]
-        mine = jnp.logical_and(other[0] == d, other[1] == t)
-
-        @pl.when(jnp.logical_not(mine))
-        def _():
-            send(src, dst, s_t1, r_t1.at[z], other)
-
-        @pl.when(mine)
-        def _():
-            pltpu.make_async_copy(src, dst, r_t1.at[z]).start()
-
+    pl.semaphore_wait(barrier, TENSOR - 1 + DP - 1)
+
+    def share_rows(s):
+        return pl.ds(pl.multiple_of(s * SHARE, SHARE), SHARE)
+
+    def to_plane(k, _):
+        s = lax.rem(t + k, TENSOR)
+        send(tokens.at[share_rows(s)], ts.at[t], s_ts, r_ts.at[t], (d, s))
         return 0
 
-    lax.fori_loop(0, DP, spread, 0)
+    pltpu.make_async_copy(tokens.at[share_rows(t)], ts.at[t], r_ts.at[t]).start()
+    lax.fori_loop(1, TENSOR, to_plane, 0)
 
     own_row = pltpu.make_async_copy(act, listed_v.at[d], l_act)
     own_row.start()
@@ -117,6 +90,30 @@
         return 0
 
     lax.fori_loop(1, DP, tell, 0)
+
+    def quarter_columns(k):
+        return pl.ds(pl.multiple_of(k * ROWS, ROWS), ROWS)
+
+    def to_rows(far):
+        wait(ts.at[far], r_ts.at[far])
+
+        def one(k, _):
+            other = far * QUARTERS + k
+
+            @pl.when(other != d)
+            def _():
+                send(ts.at[far, :, quarter_columns(k)], tok.at[xl, y, d], s_t1, r_t1.at[z], (other, t))
+
+            @pl.when(other == d)
+            def _():
+                pltpu.make_async_copy(ts.at[far, :, quarter_columns(k)], tok.at[xl, y, d], r_t1.at[z]).start()
+
+            return 0
+
+        lax.fori_loop(0, QUARTERS, one, 0)
+
+    for k in (4, -3, 3, -2, 2, -1, 1, 0):
+        to_rows(plane(k))
 
     order = [plane(k) for k in (4, 3, -3, 2, -2, 1, -1, 0)]
 
@@ -216,7 +213,7 @@
     wait(xr, r_h)
     both = acc[...] + xr[...].astype(F32)
     gate, up = both[:, : CAP * BLOCK], both[:, CAP * BLOCK :]
-    g = live_grad[...].astype(F32)
+    g = out_grad[...].astype(F32) * live[...]
     relu = jnp.maximum(gate, 0.0)
     gr[d, :, : CAP * BLOCK] = (g * up * 2.0 * relu).astype(BF16)
     gr[d, :, CAP * BLOCK :] = (g * relu * relu).astype(BF16)
@@ -301,47 +298,64 @@
 
         def home(k, _):
             q = zq * 4 + k
-            dst = out.at[pl.ds(pl.multiple_of(t * SHARE, SHARE), SHARE), pl.ds(pl.multiple_of(a * ROWS, ROWS), ROWS)]
-            mine = jnp.logical_and(q == d, at_home)
-
-            @pl.when(jnp.logical_not(mine))
+            dst = back.at[z, :, quarter_columns(a)]
+
+            @pl.when(q != d)
             def _():
-                send(fin.at[q], dst, s_o, r_o, (q, z))
-
-            @pl.when(mine)
+                send(fin.at[q], dst, s_o, r_o.at[z], (q, t))
+
+            @pl.when(q == d)
             def _():
-                pltpu.make_async_copy(fin.at[q], dst, r_o).start()
+                pltpu.make_async_copy(fin.at[q], dst, r_o.at[z]).start()
 
             return 0
 
         lax.fori_loop(0, 4, home, 0)
 
-    for e in range(NZ + 3):
-        if e == 1 or e == 3 or e == 5:
-            arrive(e // 2)
-        if e == 7:
-            arrive_last()
-        if e < NZ:
-            backward(e)
-        if 0 <= e - 1 < NZ:
-            reduce_1(e - 1)
-        if 0 <= e - 2 < NZ:
-            reduce_2(e - 2)
-        if 0 <= e - 3 < NZ:
-            reduce_3(e - 3)
-
-    wait(out, r_o)
-
-    for sem in (s_t1, s_o):
-
-        @pl.when(at_home)
+    def to_owner(e):
+        far = plane((0, 1, -1, 2, -2, 3, -3, 4)[e])
+        wait(back.at[far], r_o.at[far])
+        dst = out.at[share_rows(t)]
+
+        @pl.when(far != t)
         def _():
-            wait(fin.at[pl.ds(0, DP - 1)], sem)
-
-        @pl.when(jnp.logical_not(at_home))
+            send(back.at[far], dst, s_out, r_out, (d, far))
+
+        @pl.when(far == t)
         def _():
-            wait(fin, sem)
-
+            pltpu.make_async_copy(back.at[far], dst, r_out).start()
+
+    backward(0)
+    reduce_1(0)
+    arrive(0)
+    backward(1), backward(2)
+    reduce_2(0)
+    reduce_1(1), reduce_1(2)
+    arrive(1)
+    backward(3), backward(4)
+    reduce_3(0), reduce_2(1), reduce_2(2)
+    reduce_1(3), reduce_1(4)
+    arrive(2)
+    backward(5), backward(6)
+    reduce_3(1), reduce_3(2), reduce_2(3), reduce_2(4), to_owner(0)
+    reduce_1(5)
+    arrive_last()
+    backward(7)
+    reduce_1(6)
+    reduce_3(3), reduce_3(4), reduce_2(5)
+    reduce_1(7)
+    reduce_2(6), to_owner(1), to_owner(2)
+    reduce_2(7)
+    reduce_3(5), reduce_3(6), reduce_3(7)
+    for e in range(3, NZ):
+        to_owner(e)
+
+    wait(out, r_out)
+
+    wait(fin.at[pl.ds(0, DP - 1)], s_t1)
+    wait(fin.at[pl.ds(0, DP - 1)], s_o)
+    wait(ts.at[pl.ds(0, TENSOR - 1)], s_ts)
+    wait(ts.at[pl.ds(0, TENSOR - 1)], s_out)
     wait(listed_v.at[pl.ds(0, DP - 1)], s_act)
     wait(fin, s_x)
     wait(tok.at[0], s_y)
@@ -385,8 +399,7 @@
     width = w_gate.shape[1]
     blocks = width // BLOCK
     act = jnp.pad(jnp.minimum(active.reshape(1, CAP), blocks - 1), ((0, 0), (0, BLOCK - CAP)))
-    live = jnp.repeat(active.reshape(1, CAP) < blocks, BLOCK, axis=1)
-    live_grad = jnp.where(live, out_grad.reshape(TILE, CAP * BLOCK), 0)
+    live = jnp.repeat(active.reshape(1, CAP) < blocks, BLOCK, axis=1).astype(F32)
     vmem = pl.BlockSpec(memory_space=pltpu.VMEM)
     anywhere = pl.BlockSpec(memory_space=pl.ANY)
     dma, v = pltpu.SemaphoreType.DMA, pltpu.VMEM
@@ -394,7 +407,7 @@
     slab = (SHARE, ROWS)
     input_grad, pieces, listed = pl.pallas_call(
         main_kernel,
-        in_specs=[vmem, vmem, vmem, anywhere, anywhere],
+        in_specs=[vmem, vmem, vmem, vmem, anywhere, anywhere],
         out_specs=[vmem, anywhere, pl.BlockSpec(memory_space=pltpu.SMEM)],
         out_shape=[
             jax.ShapeDtypeStruct((TILE, QUARTERS * ROWS), BF16),
@@ -420,17 +433,20 @@
             v((2, NZ, 2, 4, *slab), BF16),
             v((NZ, 4, *slab), BF16),
             v((DP, *slab), BF16),
+            v((TENSOR, SHARE, QUARTERS * ROWS), BF16),
+            v((TENSOR, SHARE, QUARTERS * ROWS), BF16),
             dma, dma((NZ,)), dma, dma, dma, dma((2,)),
             dma, dma((NZ,)), dma, dma((2, NZ)), dma, dma((2, NZ)),
             dma, dma((NZ, 2)), dma, dma((NZ, 2)), dma, dma,
             dma, dma, dma, dma((2, 4, 2)), dma, dma((NZ, 2)),
             dma, dma((2, NZ)), dma, dma((2, NZ)), dma, dma((NZ,)),
-            dma, dma, dma,
+            dma, dma((NZ,)), dma,
+            dma, dma((NZ,)), dma, dma,
         ],
         compiler_params=pltpu.CompilerParams(
             collective_id=0, has_side_effects=True, vmem_limit_bytes=62 * 2**20
         ),
-    )(tokens, live_grad, act, w_gate, w_up)
+    )(tokens, out_grad.reshape(TILE, CAP * BLOCK), live, act, w_gate, w_up)
 
     tiles = 4
     whole = pl.BlockSpec((ROWS, width), lambda q, *_: (0, 0))
@@ -444,7 +460,7 @@
             scratch_shapes=[v((ROWS, width), F32)] * 2,
         ),
         out_shape=[jax.ShapeDtypeStruct((ROWS, width), BF16)] * 2,
-        compiler_params=pltpu.CompilerParams(vmem_limit_bytes=40 * 2**20),
+        compiler_params=pltpu.CompilerParams(vmem_limit_bytes=60 * 2**20),
     )(listed, pieces)
     return input_grad, dgate, dup
 

time: 235 us -> 199 us (0.85)
  Pallas kernels: 226 us -> 194 us
  local copies, waits for them, and re-layouts: 5.48 us -> 1.95 us
    pallas_call x1, Pallas kernels: 219 us -> 183 us  [per_device(): pl.pallas_call(main_kernel, in_specs=[vmem, vmem, vmem, vmem, anywhere, a...]
    pallas_call x1, Pallas kernels: 6.66 us -> 10.9 us  [per_device(): pl.pallas_call(sum_kernel, grid_spec=pltpu.PrefetchScalarGridSpec(num_sca...]
    unnamed x7 -> x3, local copies, waits for them, and re-layouts: 4.89 us -> 0.8 us
where the time goes in v3:
time: 199 us; the launch traced here: 198 us
  Pallas kernels  194 us (97%)
    pallas_call x1, Pallas kernels, per_device(): pl.pallas_call(main_kernel, in_specs=[vmem, vmem, vmem, vmem, anywhere, a...  183 us
    pallas_call x1, Pallas kernels, per_device(): pl.pallas_call(sum_kernel, grid_spec=pltpu.PrefetchScalarGridSpec(num_sca...  10.9 us

profile of v3, /device:TPU:7, one launch (start us, length us, event | category | flops | bytes accessed | tf_op | source)
XLA Modules:
  0.0 197.6 jit_solution(3320527032716647493)
XLA Ops:
  0.6 0.7 minimum_bitcast_fusion
  1.3 0.5 pad.4.act
  1.8 0.7 fusion
  2.5 0.6 broadcast_in_dim.3
  3.1 182.9 %shard_map.76 = (bf16[256,1024]{1,0:T(8,128)(2,1)}, bf16[32,256,512]{2,1,0:T(8,128)(2,1)}, s32[32,1,128]{2,1,0:T(1,128)}) custom-call(bf16[256,1024]{1,0:T(8,128)(2,1)} %tokens.1, bf16[256,256]{1,0:T(8,128)(2,1)} %bitcast.6, f32[1,256]{1,0:T(1,128)} %bitcast.7, s32[1,128]{1,0:T(1,128)} %pad.4.act, bf16[256,3584]{1,0:T(8,128)(2,1)} %wg_hbm.1, ...), custom_call_target="tpu_custom_call" | custom-call | tf_op jit(solution)/shard_map/pallas_call | solution.py:408
  186.0 0.0 copy-start
  186.0 10.9 %shard_map.77 = (bf16[256,3584]{1,0:T(8,128)(2,1)}, bf16[256,3584]{1,0:T(8,128)(2,1)}) custom-call(s32[32,1,128]{2,1,0:T(1,128)} %get-tuple-element.9.listed, bf16[32,256,512]{2,1,0:T(8,128)(2,1)} %get-tuple-element.10.piece_ref), custom_call_target="tpu_custom_call" | custom-call | tf_op jit(solution)/shard_map/pallas_call | solution.py:453
  196.8 0.0 copy-done
  196.8 0.8 copy.9
Async XLA Ops:
  186.0 10.9 %copy-start = (bf16[256,1024]{1,0:T(8,128)(2,1)S(1)}, bf16[256,1024]{1,0:T(8,128)(2,1)}, u32[]{:S(2)}) copy-start(bf16[256,1024]{1,0:T(8,128)(2,1)} %get-tuple-element.16) | copy-start | bytes 1572868

commit v4 on v3

--- a/solution.py
+++ b/solution.py
@@ -11,6 +11,7 @@
 ROWS = 256
 SHARE = TILE // TENSOR
 UNITS = 2 * CAP * BLOCK
+HALF = UNITS // 2
 BF16, F32 = jnp.bfloat16, jnp.float32
 
 
@@ -27,9 +28,9 @@
 def main_kernel(
     tokens, out_grad, live, act, wg_hbm, wu_hbm,
     out, pieces_hbm, listed,
-    wg, wu, listed_v, tok, sc, rc, sz, rz, xs, xr, acc, gr, part, piece, yr1, yr2, xr2, fin, ts, back,
-    s_t1, r_t1, s_act, r_act, l_act, s_w, s_x, r_x, s_y, r_y, s_f, r_f, s_c, r_c, s_z, r_z, s_h, r_h,
-    s_gh, r_gh, s_gz, r_gz, s_gc, r_gc, s_0, r_0, s_1, r_1, s_2, r_2, s_o, r_o, s_p, s_ts, r_ts, s_out, r_out,
+    wg, wu, listed_v, tok, sc, rc, sza, rza, szb, rzb, xb_s, xb_r, ch, xs, xr, gr, part, piece, yr1, yr2, xr2, fin, ts, back,
+    s_t1, r_t1, s_act, r_act, l_act, s_w, s_x, r_x, s_y, r_y, s_f, r_f, s_c, r_c, s_za, r_za, s_zb, r_zb, s_xb, r_xb, s_h, r_h,
+    s_gh, r_gh, s_gz, r_gz, s_gc, r_gc, s_0, r_0, s_1, r_1, s_2, r_2, s_o, r_o, s_p, s_ts, r_ts, s_out, r_out, s_x0, r_x0,
 ):
     d, t = lax.axis_index("dp"), lax.axis_index("tensor")
     z, a = d // QUARTERS, lax.rem(d, QUARTERS)
@@ -46,6 +47,67 @@
     y_next, y_last, y_far = lax.rem(y + 1, 4), lax.rem(y + 3, 4), lax.rem(y + 2, 4)
     up_y, down_y = (d, xl * 4 + y_next), (d, xl * 4 + y_last)
 
+    barrier = pltpu.get_barrier_semaphore()
+
+    def greet(device):
+        pl.semaphore_signal(barrier, inc=1, device_id=device, device_id_type=MESH)
+
+    def greet_dp(k, _):
+        greet((lax.rem(d + k, DP), t))
+        return 0
+
+    def greet_plane(k, _):
+        greet((d, lax.rem(t + k, TENSOR)))
+        return 0
+
+    lax.fori_loop(1, TENSOR, greet_plane, 0)
+    lax.fori_loop(1, DP, greet_dp, 0)
+    pl.semaphore_wait(barrier, TENSOR - 1 + DP - 1)
+
+    def share_rows(s):
+        return pl.ds(pl.multiple_of(s * SHARE, SHARE), SHARE)
+
+    def to_plane(k, _):
+        s = lax.rem(t + k, TENSOR)
+        send(tokens.at[share_rows(s)], ts.at[t], s_ts, r_ts.at[t], (d, s))
+        return 0
+
+    pltpu.make_async_copy(tokens.at[share_rows(t)], ts.at[t], r_ts.at[t]).start()
+    lax.fori_loop(1, TENSOR, to_plane, 0)
+
+    def quarter_columns(k):
+        return pl.ds(pl.multiple_of(k * ROWS, ROWS), ROWS)
+
+    def to_rows(far):
+        wait(ts.at[far], r_ts.at[far])
+
+        def one(k, _):
+            other = far * QUARTERS + k
+
+            @pl.when(other != d)
+            def _():
+                send(ts.at[far, :, quarter_columns(k)], tok.at[xl, y, d], s_t1, r_t1.at[z], (other, t))
+
+            @pl.when(other == d)
+            def _():
+                pltpu.make_async_copy(ts.at[far, :, quarter_columns(k)], tok.at[xl, y, d], r_t1.at[z]).start()
+
+            return 0
+
+        lax.fori_loop(0, QUARTERS, one, 0)
+
+    for k in (4, -3, 3, -2, 2, -1, 1, 0):
+        to_rows(plane(k))
+
+    own_row = pltpu.make_async_copy(act, listed_v.at[d], l_act)
+    own_row.start()
+
+    def tell(k, _):
+        send(act, listed_v.at[d], s_act, r_act, (lax.rem(d + k, DP), t))
+        return 0
+
+    lax.fori_loop(1, DP, tell, 0)
+
     def load_block(b, _):
         columns = pl.ds(pl.multiple_of(b * BLOCK, BLOCK), BLOCK)
         pltpu.make_async_copy(wg_hbm.at[:, columns], wg.at[b], s_w.at[0]).start()
@@ -54,71 +116,20 @@
 
     lax.fori_loop(0, wg.shape[0], load_block, 0)
 
-    barrier = pltpu.get_barrier_semaphore()
-
-    def greet(device):
-        pl.semaphore_signal(barrier, inc=1, device_id=device, device_id_type=MESH)
-
-    def greet_dp(k, _):
-        greet((lax.rem(d + k, DP), t))
-        return 0
-
-    def greet_plane(k, _):
-        greet((d, lax.rem(t + k, TENSOR)))
-        return 0
-
-    lax.fori_loop(1, TENSOR, greet_plane, 0)
-    lax.fori_loop(1, DP, greet_dp, 0)
-    pl.semaphore_wait(barrier, TENSOR - 1 + DP - 1)
-
-    def share_rows(s):
-        return pl.ds(pl.multiple_of(s * SHARE, SHARE), SHARE)
-
-    def to_plane(k, _):
-        s = lax.rem(t + k, TENSOR)
-        send(tokens.at[share_rows(s)], ts.at[t], s_ts, r_ts.at[t], (d, s))
-        return 0
-
-    pltpu.make_async_copy(tokens.at[share_rows(t)], ts.at[t], r_ts.at[t]).start()
-    lax.fori_loop(1, TENSOR, to_plane, 0)
-
-    own_row = pltpu.make_async_copy(act, listed_v.at[d], l_act)
-    own_row.start()
-
-    def tell(k, _):
-        send(act, listed_v.at[d], s_act, r_act, (lax.rem(d + k, DP), t))
-        return 0
-
-    lax.fori_loop(1, DP, tell, 0)
-
-    def quarter_columns(k):
-        return pl.ds(pl.multiple_of(k * ROWS, ROWS), ROWS)
-
-    def to_rows(far):
-        wait(ts.at[far], r_ts.at[far])
-
-        def one(k, _):
-            other = far * QUARTERS + k
-
-            @pl.when(other != d)
-            def _():
-                send(ts.at[far, :, quarter_columns(k)], tok.at[xl, y, d], s_t1, r_t1.at[z], (other, t))
-
-            @pl.when(other == d)
-            def _():
-                pltpu.make_async_copy(ts.at[far, :, quarter_columns(k)], tok.at[xl, y, d], r_t1.at[z]).start()
-
-            return 0
-
-        lax.fori_loop(0, QUARTERS, one, 0)
-
-    for k in (4, -3, 3, -2, 2, -1, 1, 0):
-        to_rows(plane(k))
-
     order = [plane(k) for k in (4, 3, -3, 2, -2, 1, -1, 0)]
 
     def four(zq):
         return pl.ds(zq * 4, 4)
+
+    def stage_all(o):
+        mine = tok.at[xl, y, four(order[o])]
+        wait(mine, r_t1.at[order[o]])
+
+        def one(k, _):
+            send(mine, mine, s_x0, r_x0, (d, lax.rem(t + k, TENSOR)))
+            return 0
+
+        lax.fori_loop(1, TENSOR, one, 0)
 
     def stage_x(o):
         mine = tok.at[xl, y, four(order[o])]
@@ -148,18 +159,15 @@
     def partial_sum(q):
         return jnp.dot(tile_tokens(q), tile_weights(q), preferred_element_type=F32)
 
-    def settle(o, k, received):
-        total = partial_sum(order[o] * 4 + k * 2 + c)
-        wait(rc.at[o, k], r_c.at[o, k])
-        total = total + rc[o, k].astype(F32)
-        for slot in received:
-            wait(rz.at[slot, k], r_z.at[slot, k])
-            total = total + rz[slot, k].astype(F32)
-        return total
-
-    def stage_c(o):
-        wait(tok.at[:, y_far, pl.ds(order[o] * 4, 2)], r_f.at[0, o])
-        wait(tok.at[:, y_far, pl.ds(order[o] * 4 + 2, 2)], r_f.at[1, o])
+    def along(o):
+        return up_z if o % 2 else down_z
+
+    def chip_sum(o):
+        if o == 0:
+            wait(fin.at[pl.ds(0, 4 * (TENSOR - 1))], r_x0)
+        else:
+            wait(tok.at[:, y_far, pl.ds(order[o] * 4, 2)], r_f.at[0, o])
+            wait(tok.at[:, y_far, pl.ds(order[o] * 4 + 2, 2)], r_f.at[1, o])
 
         def for_sibling(k, _):
             sc[o, k] = partial_sum(order[o] * 4 + k * 2 + 1 - c).astype(BF16)
@@ -167,52 +175,107 @@
             return 0
 
         lax.fori_loop(0, 2, for_sibling, 0)
+
+        def for_me(k, _):
+            ch[o % 2, k] = partial_sum(order[o] * 4 + k * 2 + c)
+            return 0
+
+        lax.fori_loop(0, 2, for_me, 0)
+
+    def join(o):
+        for k in (1 - xh, xh):
+            wait(rc.at[o, k], r_c.at[o, k])
+            ch[o % 2, k] += rc[o, k].astype(F32)
+            if k is not xh:
+                xb_s[o] = ch[o % 2, k, :, HALF:].astype(BF16)
+                send(xb_s.at[o], xb_r.at[o], s_xb, r_xb.at[o], across)
+
+    def gate_sum(o, k, slots):
+        total = ch[o % 2, k, :, :HALF]
+        for slot in slots:
+            wait(rza.at[slot, k], r_za.at[slot, k])
+            total = total + rza[slot, k].astype(F32)
+        return total
+
+    def up_sum(o, slots, rows):
+        total = ch[o % 2, xh, rows, HALF:] + xb_r[o, rows].astype(F32)
+        for slot in slots:
+            wait(rzb.at[slot, rows], r_zb.at[slot])
+            total = total + rzb[slot, rows].astype(F32)
+        return total
+
+    top, bottom, full = pl.ds(0, TILE // 2), pl.ds(TILE // 2, TILE // 2), pl.ds(0, TILE)
+
+    def ring(o):
         if o == 0:
-            for k, slot, device in ((0, 0, up_z), (1, 1, down_z)):
-                sz[o, k] = settle(o, k, ()).astype(BF16)
-                send(sz.at[o, k], rz.at[slot, k], s_z, r_z.at[slot, k], device)
-        elif o <= 2:
-            device = up_z if o == 1 else down_z
+            for k, device in ((0, up_z), (1, down_z)):
+                sza[o, k] = gate_sum(o, k, ()).astype(BF16)
+                send(sza.at[o, k], rza.at[k, k], s_za, r_za.at[k, k], device)
+            wait(xb_r.at[o], r_xb.at[o])
+            for k, device, rows in ((0, up_z, top), (1, down_z, bottom)):
+                szb[o, rows] = up_sum(o, (), rows).astype(BF16)
+                send(szb.at[o, rows], rzb.at[k, rows], s_zb, r_zb.at[k], device)
+            return
+        device, slot = along(o), o + 1
+        if o <= 2:
             for k in (o - 1, 2 - o):
-                sz[o, k] = settle(o, k, (o - 1,) if k == o - 1 else ()).astype(BF16)
-                send(sz.at[o, k], rz.at[o + 1, k], s_z, r_z.at[o + 1, k], device)
+                sza[o, k] = gate_sum(o, k, (o - 1,) if k == o - 1 else ()).astype(BF16)
+                send(sza.at[o, k], rza.at[slot, k], s_za, r_za.at[slot, k], device)
+            wait(xb_r.at[o], r_xb.at[o])
+            for k, rows in ((0, top), (1, bottom)):
+                szb[o, rows] = up_sum(o, (o - 1,) if k == o - 1 else (), rows).astype(BF16)
+            send(szb.at[o], rzb.at[slot], s_zb, r_zb.at[slot], device)
         elif o <= 6:
-            device = up_z if o % 2 else down_z
-
-            def along(k, _):
-                sz[o, k] = settle(o, k, (o - 1,)).astype(BF16)
-                send(sz.at[o, k], rz.at[o + 1, k], s_z, r_z.at[o + 1, k], device)
+
+            def one(k, _):
+                sza[o, k] = gate_sum(o, k, (o - 1,)).astype(BF16)
+                send(sza.at[o, k], rza.at[slot, k], s_za, r_za.at[slot, k], device)
                 return 0
 
-            lax.fori_loop(0, 2, along, 0)
+            lax.fori_loop(0, 2, one, 0)
+            wait(xb_r.at[o], r_xb.at[o])
+            szb[o] = up_sum(o, (o - 1,), full).astype(BF16)
+            send(szb.at[o], rzb.at[slot], s_zb, r_zb.at[slot], device)
         else:
-            xs[...] = settle(o, 1 - xh, (6, 7)).astype(BF16)
+            xs[...] = gate_sum(o, 1 - xh, (6, 7)).astype(BF16)
             send(xs, xr, s_h, r_h, across)
-            acc[...] = settle(o, xh, (6, 7))
-
+            ch[o % 2, xh, :, :HALF] = gate_sum(o, xh, (6, 7))
+            wait(xb_r.at[o], r_xb.at[o])
+            ch[o % 2, xh, :, HALF:] = up_sum(o, (6, 7), full)
+
+    stage_all(0)
+    stage_x(1)
+    stage_x(2)
+    stage_y(1)
+    stage_x(3)
+    wait(wg, s_w.at[0])
+    wait(wu, s_w.at[1])
+    own_row.wait()
+    wait(listed_v.at[pl.ds(0, DP - 1)], r_act)
+    to_smem = pltpu.make_async_copy(listed_v, listed, l_act)
+    to_smem.start()
+    to_smem.wait()
     for o in range(NZ):
-        stage_x(o)
+        if 0 < o and o + 2 < NZ:
+            stage_y(o + 2)
+        if 0 < o and o + 3 < NZ:
+            stage_x(o + 3)
+        if 0 < o < NZ - 1:
+            stage_f(o + 1)
+        chip_sum(o)
         if o == 0:
-            wait(wg, s_w.at[0])
-            wait(wu, s_w.at[1])
-            own_row.wait()
-            wait(listed_v.at[pl.ds(0, DP - 1)], r_act)
-            to_smem = pltpu.make_async_copy(listed_v, listed, l_act)
-            to_smem.start()
-            to_smem.wait()
-    for o in range(3):
-        stage_y(o)
-    stage_f(0)
-    for o in range(NZ):
-        if o + 3 < NZ:
-            stage_y(o + 3)
-        if o + 1 < NZ:
-            stage_f(o + 1)
-        stage_c(o)
+            stage_f(1)
+            stage_y(2)
+        if o > 1:
+            ring(o - 1)
+        join(o)
+        if o == 0:
+            ring(0)
+    ring(NZ - 1)
 
     wait(xr, r_h)
-    both = acc[...] + xr[...].astype(F32)
-    gate, up = both[:, : CAP * BLOCK], both[:, CAP * BLOCK :]
+    gate = ch[(NZ - 1) % 2, xh, :, :HALF] + xr[...].astype(F32)
+    up = ch[(NZ - 1) % 2, xh, :, HALF:]
     g = out_grad[...].astype(F32) * live[...]
     relu = jnp.maximum(gate, 0.0)
     gr[d, :, : CAP * BLOCK] = (g * up * 2.0 * relu).astype(BF16)
@@ -357,11 +420,15 @@
     wait(ts.at[pl.ds(0, TENSOR - 1)], s_ts)
     wait(ts.at[pl.ds(0, TENSOR - 1)], s_out)
     wait(listed_v.at[pl.ds(0, DP - 1)], s_act)
-    wait(fin, s_x)
-    wait(tok.at[0], s_y)
-    wait(tok.at[0, pl.ds(0, 2)], s_f)
+    most = pl.ds(0, 4 * (NZ - 1))
+    wait(fin.at[most], s_x0)
+    wait(fin.at[most], s_x)
+    wait(tok.at[0, :, most], s_y)
+    wait(tok.at[0, pl.ds(0, 2), most], s_f)
     wait(sc, s_c)
-    wait(sz, s_z)
+    wait(sza, s_za)
+    wait(szb, s_zb)
+    wait(xb_s, s_xb)
     wait(xs, s_h)
     wait(gr.at[d], s_gh)
     wait(gr.at[pl.ds(0, 14)], s_gz)
@@ -372,27 +439,45 @@
     wait(piece, s_p)
 
 
-def sum_kernel(listed, piece_ref, dgate_ref, dup_ref, gate_acc, up_acc):
-    step = pl.program_id(0)
-    tiles = piece_ref.shape[0]
-
-    @pl.when(step == 0)
+def sum_kernel(listed, piece_ref, dgate_ref, dup_ref, count, slots):
+    blocks = dgate_ref.shape[1] // BLOCK
+    chunk = piece_ref.shape[1]
+
+    @pl.when(pl.program_id(0) == 0)
     def _():
-        gate_acc[...] = jnp.zeros_like(gate_acc)
-        up_acc[...] = jnp.zeros_like(up_acc)
-
-    for k in range(tiles):
-        for c in range(CAP):
-            block = listed[step * tiles + k, 0, c]
-            at = pl.ds(pl.multiple_of(block * BLOCK, BLOCK), BLOCK)
-            for m, acc in enumerate((gate_acc, up_acc)):
-                column = (m * CAP + c) * BLOCK
-                acc[:, at] += piece_ref[k, :, column : column + BLOCK].astype(F32)
-
-    @pl.when(step == pl.num_programs(0) - 1)
-    def _():
-        dgate_ref[...] = gate_acc[...].astype(BF16)
-        dup_ref[...] = up_acc[...].astype(BF16)
+        def clear(b, _):
+            count[b] = 0
+            return 0
+
+        lax.fori_loop(0, blocks, clear, 0)
+
+        def enter(s, _):
+            block = listed[s // CAP, 0, lax.rem(s, CAP)]
+            at = count[block]
+            slots[block * (DP * CAP) + at] = s
+            count[block] = at + 1
+            return 0
+
+        lax.fori_loop(0, DP * CAP, enter, 0)
+
+    def one_block(b, _):
+        def add(i, sums):
+            s = slots[b * (DP * CAP) + i]
+            q, c = s // CAP, lax.rem(s, CAP)
+            new = []
+            for k, total in enumerate(sums):
+                at = pl.ds(pl.multiple_of((k * CAP + c) * BLOCK, BLOCK), BLOCK)
+                new.append(total + piece_ref[q, :, at].astype(F32))
+            return tuple(new)
+
+        nothing = jnp.zeros((chunk, BLOCK), F32)
+        sums = lax.fori_loop(0, count[b], add, (nothing, nothing))
+        at = pl.ds(pl.multiple_of(b * BLOCK, BLOCK), BLOCK)
+        dgate_ref[:, at] = sums[0].astype(BF16)
+        dup_ref[:, at] = sums[1].astype(BF16)
+        return 0
+
+    lax.fori_loop(0, blocks, one_block, 0)
 
 
 def per_device(tokens, out_grad, active, w_gate, w_up):
@@ -421,11 +506,15 @@
             v((2, 4, DP, *slab), BF16),
             v((NZ, 2, *tile), BF16),
             v((NZ, 2, *tile), BF16),
-            v((NZ - 1, 2, *tile), BF16),
-            v((NZ, 2, *tile), BF16),
-            v(tile, BF16),
-            v(tile, BF16),
-            v(tile, F32),
+            v((NZ - 1, 2, TILE, HALF), BF16),
+            v((NZ, 2, TILE, HALF), BF16),
+            v((NZ - 1, TILE, HALF), BF16),
+            v((NZ, TILE, HALF), BF16),
+            v((NZ, TILE, HALF), BF16),
+            v((NZ, TILE, HALF), BF16),
+            v((2, 2, *tile), F32),
+            v((TILE, HALF), BF16),
+            v((TILE, HALF), BF16),
             v((DP, *tile), BF16),
             v((2, 4, DP, *slab), BF16),
             v((DP, ROWS, UNITS), BF16),
@@ -437,27 +526,28 @@
             v((TENSOR, SHARE, QUARTERS * ROWS), BF16),
             dma, dma((NZ,)), dma, dma, dma, dma((2,)),
             dma, dma((NZ,)), dma, dma((2, NZ)), dma, dma((2, NZ)),
-            dma, dma((NZ, 2)), dma, dma((NZ, 2)), dma, dma,
+            dma, dma((NZ, 2)), dma, dma((NZ, 2)), dma, dma((NZ,)), dma, dma((NZ,)), dma, dma,
             dma, dma, dma, dma((2, 4, 2)), dma, dma((NZ, 2)),
             dma, dma((2, NZ)), dma, dma((2, NZ)), dma, dma((NZ,)),
             dma, dma((NZ,)), dma,
             dma, dma((NZ,)), dma, dma,
+            dma, dma,
         ],
         compiler_params=pltpu.CompilerParams(
             collective_id=0, has_side_effects=True, vmem_limit_bytes=62 * 2**20
         ),
     )(tokens, out_grad.reshape(TILE, CAP * BLOCK), live, act, w_gate, w_up)
 
-    tiles = 4
-    whole = pl.BlockSpec((ROWS, width), lambda q, *_: (0, 0))
+    chunk = 128
+    some_rows = pl.BlockSpec((chunk, width), lambda r, *_: (r, 0))
     dgate, dup = pl.pallas_call(
         sum_kernel,
         grid_spec=pltpu.PrefetchScalarGridSpec(
             num_scalar_prefetch=1,
-            grid=(DP // tiles,),
-            in_specs=[pl.BlockSpec((tiles, ROWS, UNITS), lambda q, *_: (q, 0, 0))],
-            out_specs=[whole, whole],
-            scratch_shapes=[v((ROWS, width), F32)] * 2,
+            grid=(ROWS // chunk,),
+            in_specs=[pl.BlockSpec((DP, chunk, UNITS), lambda r, *_: (0, r, 0))],
+            out_specs=[some_rows, some_rows],
+            scratch_shapes=[pltpu.SMEM((blocks,), jnp.int32), pltpu.SMEM((blocks * DP * CAP,), jnp.int32)],
         ),
         out_shape=[jax.ShapeDtypeStruct((ROWS, width), BF16)] * 2,
         compiler_params=pltpu.CompilerParams(vmem_limit_bytes=60 * 2**20),

time: 199 us -> 186 us (0.935)
  Pallas kernels: 194 us -> 182 us
    pallas_call x1, Pallas kernels: 183 us -> 173 us  [per_device(): pl.pallas_call(main_kernel, in_specs=[vmem, vmem, vmem, vmem, anywhere, a...]
where the time goes in v4:
time: 186 us
  Pallas kernels  182 us (98%)
  local copies, waits for them, and re-layouts  1.95 us (1%)
    pallas_call x1, Pallas kernels, per_device(): pl.pallas_call(main_kernel, in_specs=[vmem, vmem, vmem, vmem, anywhere, a...  173 us
    pallas_call x1, Pallas kernels, per_device(): pl.pallas_call(sum_kernel, grid_spec=pltpu.PrefetchScalarGridSpec(num_sca...  9.15 us

profile of v4, /device:TPU:7, one launch (start us, length us, event | category | flops | bytes accessed | tf_op | source)
XLA Modules:
  0.0 186.0 jit_solution(623536025676814271)
XLA Ops:
  0.6 0.7 minimum_bitcast_fusion
  1.3 0.5 pad.4.act
  1.8 0.7 fusion
  2.5 0.6 broadcast_in_dim.3
  3.1 172.9 %shard_map.76 = (bf16[256,1024]{1,0:T(8,128)(2,1)}, bf16[32,256,512]{2,1,0:T(8,128)(2,1)}, s32[32,1,128]{2,1,0:T(1,128)}) custom-call(bf16[256,1024]{1,0:T(8,128)(2,1)} %tokens.1, bf16[256,256]{1,0:T(8,128)(2,1)} %bitcast.6, f32[1,256]{1,0:T(1,128)} %bitcast.7, s32[1,128]{1,0:T(1,128)} %pad.4.act, bf16[256,3584]{1,0:T(8,128)(2,1)} %wg_hbm.1, ...), custom_call_target="tpu_custom_call" | custom-call | tf_op jit(solution)/shard_map/pallas_call | solution.py:493
  176.0 0.0 copy-start
  176.1 9.2 %shard_map.77 = (bf16[256,3584]{1,0:T(8,128)(2,1)}, bf16[256,3584]{1,0:T(8,128)(2,1)}) custom-call(s32[32,1,128]{2,1,0:T(1,128)} %get-tuple-element.9.listed, bf16[32,256,512]{2,1,0:T(8,128)(2,1)} %get-tuple-element.10.piece_ref), custom_call_target="tpu_custom_call" | custom-call | tf_op jit(solution)/shard_map/pallas_call | solution.py:543
  185.2 0.0 copy-done
  185.2 0.8 copy.9
Async XLA Ops:
  176.0 9.2 %copy-start = (bf16[256,1024]{1,0:T(8,128)(2,1)S(1)}, bf16[256,1024]{1,0:T(8,128)(2,1)}, u32[]{:S(2)}) copy-start(bf16[256,1024]{1,0:T(8,128)(2,1)} %get-tuple-element.16) | copy-start | bytes 1572868

commit v5 on v4

--- a/solution.py
+++ b/solution.py
@@ -318,6 +318,22 @@
             wait(own(arrivals[7], k), r_gz.at[k, 3, k])
             to_sibling(7, arrivals[7], k)
 
+    late = 5
+
+    def piece_of(q, grads):
+        value = lax.dot_general(tile_tokens(q), grads, (((0,), (0,)), ((), ())), preferred_element_type=F32)
+        piece[q] = value.astype(BF16)
+
+    def pieces(e):
+        zq = arrivals[e]
+
+        def one(k, _):
+            piece_of(zq * 4 + k, gr[zq * 4 + k])
+            return 0
+
+        lax.fori_loop(0, 4, one, 0)
+        pltpu.make_async_copy(piece.at[four(zq)], pieces_hbm.at[four(zq)], s_p).start()
+
     def backward(e):
         zq = arrivals[e]
         for k in (0, 1):
@@ -328,12 +344,13 @@
             grads = gr[q]
             value = lax.dot_general(grads, tile_weights(q), (((1,), (1,)), ((), ())), preferred_element_type=F32)
             part[:, :, q] = value.astype(BF16).reshape(2, 4, SHARE, ROWS)
-            value = lax.dot_general(tile_tokens(q), grads, (((0,), (0,)), ((), ())), preferred_element_type=F32)
-            piece[q] = value.astype(BF16)
+            if e < late:
+                piece_of(q, grads)
             return 0
 
         lax.fori_loop(0, 4, one, 0)
-        pltpu.make_async_copy(piece.at[four(zq)], pieces_hbm.at[four(zq)], s_p).start()
+        if e < late:
+            pltpu.make_async_copy(piece.at[four(zq)], pieces_hbm.at[four(zq)], s_p).start()
         first, second = pl.ds(zq * 4, 2), pl.ds(zq * 4 + 2, 2)
         send(part.at[:, y_far, first], yr1.at[0, e], s_0, r_0.at[0, e], up_y)
         send(part.at[:, y_far, second], yr1.at[1, e], s_0, r_0.at[1, e], down_y)
@@ -407,9 +424,13 @@
     reduce_1(6)
     reduce_3(3), reduce_3(4), reduce_2(5)
     reduce_1(7)
+    pieces(5)
     reduce_2(6), to_owner(1), to_owner(2)
+    pieces(6)
     reduce_2(7)
-    reduce_3(5), reduce_3(6), reduce_3(7)
+    reduce_3(5), reduce_3(6)
+    pieces(7)
+    reduce_3(7)
     for e in range(3, NZ):
         to_owner(e)
 

time: 186 us -> 186 us (level)
  no operation moved by 1% of the time
where the time goes in v5:
time: 186 us; the launch traced here: 185 us
  Pallas kernels  181 us (97%)
  local copies, waits for them, and re-layouts  1.95 us (1%)
    pallas_call x1, Pallas kernels, per_device(): pl.pallas_call(main_kernel, in_specs=[vmem, vmem, vmem, vmem, anywhere, a...  172 us
    pallas_call x1, Pallas kernels, per_device(): pl.pallas_call(sum_kernel, grid_spec=pltpu.PrefetchScalarGridSpec(num_sca...  9.16 us

profile of v5, /device:TPU:7, one launch (start us, length us, event | category | flops | bytes accessed | tf_op | source)
XLA Modules:
  0.0 185.3 jit_solution(12679953038207201830)
XLA Ops:
  0.6 0.7 minimum_bitcast_fusion
  1.3 0.5 pad.4.act
  1.8 0.7 fusion
  2.5 0.6 broadcast_in_dim.3
  3.1 172.2 %shard_map.76 = (bf16[256,1024]{1,0:T(8,128)(2,1)}, bf16[32,256,512]{2,1,0:T(8,128)(2,1)}, s32[32,1,128]{2,1,0:T(1,128)}) custom-call(bf16[256,1024]{1,0:T(8,128)(2,1)} %tokens.1, bf16[256,256]{1,0:T(8,128)(2,1)} %bitcast.6, f32[1,256]{1,0:T(1,128)} %bitcast.7, s32[1,128]{1,0:T(1,128)} %pad.4.act, bf16[256,3584]{1,0:T(8,128)(2,1)} %wg_hbm.1, ...), custom_call_target="tpu_custom_call" | custom-call | tf_op jit(solution)/shard_map/pallas_call | solution.py:514
  175.3 0.0 copy-start
  175.3 9.2 %shard_map.77 = (bf16[256,3584]{1,0:T(8,128)(2,1)}, bf16[256,3584]{1,0:T(8,128)(2,1)}) custom-call(s32[32,1,128]{2,1,0:T(1,128)} %get-tuple-element.9.listed, bf16[32,256,512]{2,1,0:T(8,128)(2,1)} %get-tuple-element.10.piece_ref), custom_call_target="tpu_custom_call" | custom-call | tf_op jit(solution)/shard_map/pallas_call | solution.py:564
  184.5 0.0 copy-done
  184.5 0.8 copy.9
Async XLA Ops:
  175.3 9.2 %copy-start = (bf16[256,1024]{1,0:T(8,128)(2,1)S(1)}, bf16[256,1024]{1,0:T(8,128)(2,1)}, u32[]{:S(2)}) copy-start(bf16[256,1024]{1,0:T(8,128)(2,1)} %get-tuple-element.16) | copy-start | bytes 1572868
